TPU v7x, 32 devices: a whole 2x2x4 slice. The times are simulated.
32 devices in a mesh: front: 4 (over x, core), wide: 8 (over z, y).
Axes of the slice: x: 2, y: 2, z: 4, core: 2. Of those that a mesh axis runs over, the one named last changes fastest.
Arguments:
- inv_diag: bfloat16 [4, 8192, 8192], P('front', 'wide'), as said below
- below: bfloat16 [4, 6144, 8192], P('front', 'wide'), may hold values from -0.0625 to 0.0625
- rhs: bfloat16 [4, 8192, 256], P('front', 'wide'), may hold values from -6 to 6
- tile_count: int32 [4], replicated, may hold values from 36 to 48, as said below
- tile_owner: int32 [4, 48, 1], P('front', 'wide'), may hold values from 0 to 3; in each aligned block of 6 rows (0 to 5, 6 to 11, ..., all dimensions but the last counted through in order) at most 2 rows name the same one
- tile_rows: int32 [4, 48, 128], P('front', 'wide'), may hold values from 0 to 511
- parent_rhs: bfloat16 [4, 4096, 256], P('front', 'wide'), may hold values from -6 to 6
Outputs:
- solved: bfloat16 [4, 8192, 256], P('front', 'wide')
- parent_new: float32 [4, 4096, 256], P('front', 'wide')
Inputs may be any that keep to these rules, and one draw needn't show every extreme that they name: Each inv_diag[f] is lower triangular. Tiles of front f with index at least tile_count[f] carry nothing; some front has all 48 tiles live. `tile_owner`: among the 6 tiles of one device (aligned blocks of tiles), no front index is named more than 2 times.
All inputs are finite; a program needn't handle non-finite values.
Results may differ from a plain program's by a relative error of at most 0.0037.
Values may be sent and summed in bfloat16 or wider, within the bound.
No kernel may reach another device: no remote copies, remote signals or barrier semaphores. Data moves between devices by JAX's collectives and lax.ppermute only.
A program may use at most 128 MiB of HBM per device.

v0:
```python
import jax
import jax.numpy as jnp
from jax import lax
from jax.experimental.layout import Layout, with_layout_constraint
from jax.sharding import PartitionSpec as P

CAPACITY = 2
BASE = 256
LANES = 128
DEPTH = 4


def row_major(array):
    return with_layout_constraint(array, Layout(major_to_minor=tuple(range(array.ndim))))


def dot(a, b):
    return row_major(jnp.dot(a, b, preferred_element_type=jnp.float32))


def body(inv_diag, below, rhs, tile_count, tile_owner, tile_rows, parent_rhs):
    width = rhs.shape[2]
    rows = rhs.shape[1]
    tiles = tile_owner.shape[1]
    height = tile_rows.shape[2]
    parent_height = parent_rhs.shape[1]
    fronts = lax.axis_size("front")
    wide = lax.axis_size("wide")
    me = lax.axis_index("front")
    wide_index = lax.axis_index("wide")
    depth = DEPTH if wide % DEPTH == 0 else 1
    across = wide // depth
    z, y = wide_index // across, wide_index % across
    z_ring = [(i, (i + across) % wide) for i in range(wide)]
    y_shifts = [
        [(i, i // across * across + (i + shift) % across) for i in range(wide)]
        for shift in range(across)
    ]

    def block_of(step, shift):
        return (z + depth - step) % depth * across + (y + across - shift) % across

    def part(matrix, step, shift, values):
        columns = lax.dynamic_slice_in_dim(matrix, block_of(step, shift) * rows, rows, 1)
        return dot(columns, values)

    def gathered_product(matrix, blocks):
        column_count = len(blocks)
        total = part(matrix, 0, 0, jnp.concatenate(blocks, axis=1))
        waiting = []
        following = list(blocks)
        for step in range(depth):
            held_now = following
            if step:
                held_now[0], total = lax.optimization_barrier((held_now[0], total))
            following = [lax.ppermute(b, "wide", z_ring) for b in held_now] if step < depth - 1 else None
            passed = [
                [lax.ppermute(b, "wide", y_shifts[shift]) for b in held_now]
                for shift in range(1, across)
            ]
            if step:
                total = total + part(matrix, step, 0, jnp.concatenate(held_now, axis=1))
            for at, shift, pieces in waiting:
                total = total + part(matrix, at, shift, jnp.concatenate(pieces, axis=1))
            waiting = [(step, shift, passed[shift - 1]) for shift in range(1, across)]
        results = []
        for column in range(column_count):
            piece = total[:, column * LANES:(column + 1) * LANES]
            for at, shift, pieces in waiting:
                piece = piece + part(matrix, at, shift, pieces[column])
            results.append(piece.astype(jnp.bfloat16))
        return results

    swaps = [[(i, i ^ delta) for i in range(fronts)] for delta in range(fronts)]
    serial = jnp.arange(tiles, dtype=jnp.int32)
    live_count = jnp.sum(jnp.where(jnp.arange(fronts) == me, tile_count, 0))
    alive = wide_index * tiles + serial < live_count
    owners = tile_owner[0, :, 0]
    same_owner = owners[:, None] == owners[None, :]
    earlier = serial[None, :] < serial[:, None]
    slot = jnp.sum((same_owner & earlier).astype(jnp.int32), axis=1)
    slots = fronts * CAPACITY
    seat = jnp.where(alive, (owners ^ me) * CAPACITY + slot, slots)
    chosen = jnp.arange(slots, dtype=jnp.int32)[:, None] == seat[None, :]
    shifted = tile_rows[0] - parent_height
    rows_out = parent_height + jnp.sum(jnp.where(chosen[:, :, None], shifted[None], 0), axis=1)
    digits = jnp.stack(
        [
            (rows_out // BASE).reshape(fronts, CAPACITY, height),
            (rows_out % BASE).reshape(fronts, CAPACITY, height),
        ],
        axis=1,
    ).astype(jnp.bfloat16).reshape(fronts, 2 * CAPACITY, height)
    digits = jnp.pad(digits, ((0, 0), (0, 16 - 2 * CAPACITY), (0, 0)))
    picker = (
        jnp.arange(slots * height, dtype=jnp.int32)[:, None]
        == (seat[:, None] * height + jnp.arange(height, dtype=jnp.int32)[None, :]).reshape(1, -1)
    ).astype(jnp.bfloat16)
    picker = picker.reshape(fronts, CAPACITY * height, tiles * height)

    cuts = range(0, width, LANES)
    solved = gathered_product(inv_diag[0], [rhs[0][:, c:c + LANES] for c in cuts])
    numbers = jnp.arange(parent_height, dtype=jnp.int32)[:, None]

    updates = gathered_product(below[0], solved)
    tall = CAPACITY * height
    hits = [None] * fronts
    results = []
    for c, update in zip(cuts, updates):
        total = parent_rhs[0][:, c:c + LANES].astype(jnp.float32)
        for delta in range(fronts):
            values = dot(picker[delta], update).astype(jnp.bfloat16)
            if c == 0:
                values = jnp.concatenate([values, digits[delta]], axis=0)
            if delta:
                values = lax.ppermute(values, "front", swaps[delta])
            if c == 0:
                pair = values[tall:tall + 2 * CAPACITY].astype(jnp.float32).astype(jnp.int32)
                places = (pair[:CAPACITY] * BASE + pair[CAPACITY:]).reshape(1, -1)
                hits[delta] = (numbers == places).astype(jnp.bfloat16)
            total = total - dot(hits[delta], values[:tall])
        results.append(total)
    return (
        jnp.concatenate(solved, axis=1)[None],
        jnp.concatenate(results, axis=1)[None],
    )


def solution(mesh):
    split = P("front", "wide", None)
    return jax.shard_map(
        body,
        mesh=mesh,
        in_specs=(split, split, split, P(), split, split, split),
        out_specs=(split, split),
        check_vma=False,
    )
```

profile of v0, /device:TPU:0, one launch (start us, length us, event | category | flops | bytes accessed | tf_op | source)
XLA Modules:
  0.0 112.7 jit_solution(10711428966927754036)
XLA Ops:
  0.6 1.1 fusion.210
  1.7 3.1 %collective-permute-start = (bf16[1024,128]{1,0:T(8,128)(2,1)S(1)}, bf16[1024,128]{1,0:T(8,128)(2,1)S(1)}, u32[]{:S(2)}, u32[]{:S(2)}) collective-permute-start(bf16[1024,128]{1,0:T(8,128)(2,1)S(1)} %get-tuple-element.28), channel_id=1, source_target_pairs={{0,2},{1,3},{2,4},{3,5},{4,6},{5,7},{6,0},{7,1},{8,10},{9,11},{10,... | collective-permute-start | bytes 786440 | tf_op jit(solution)/shard_map/ppermute | solution.py:56
  4.8 1.5 %collective-permute-start.3 = (bf16[1024,128]{1,0:T(8,128)(2,1)S(1)}, bf16[1024,128]{1,0:T(8,128)(2,1)S(1)}, u32[]{:S(2)}, u32[]{:S(2)}) collective-permute-start(bf16[1024,128]{1,0:T(8,128)(2,1)S(1)} %get-tuple-element.28), channel_id=1, source_target_pairs={{0,1},{1,0},{2,3},{3,2},{4,5},{5,4},{6,7},{7,6},{8,9},{9,8},{10,11... | collective-permute-start | bytes 786440 | tf_op jit(solution)/shard_map/ppermute | solution.py:58
  6.3 1.6 %collective-permute-start.2 = (bf16[1024,128]{1,0:T(8,128)(2,1)S(1)}, bf16[1024,128]{1,0:T(8,128)(2,1)S(1)}, u32[]{:S(2)}, u32[]{:S(2)}) collective-permute-start(bf16[1024,128]{1,0:T(8,128)(2,1)S(1)} %get-tuple-element.29), channel_id=1, source_target_pairs={{0,2},{1,3},{2,4},{3,5},{4,6},{5,7},{6,0},{7,1},{8,10},{9,11},{10,... | collective-permute-start | bytes 786440 | tf_op jit(solution)/shard_map/ppermute | solution.py:56
  8.4 0.9 convert_reduce_fusion
  9.3 1.3 %fusion.195 = s32[]{:T(128)} fusion(s32[4]{0:T(128)} %param.10, s32[]{:T(128)S(6)} %axis_index.25), kind=kLoop, calls=%fused_computation.214 | loop fusion | flops 11 | bytes 24 | tf_op jit(solution)/shard_map/reduce_sum | solution.py:76
  10.6 1.3 %broadcast_multiply_fusion = (s32[6]{0:T(128)S(1)}, s32[6]{0:T(128)S(1)}) fusion(s32[6]{0:T(128)S(1)} %convert_reduce_fusion, s32[]{:T(128)S(6)} %axis_index.25, s32[1,6,1]{1,2,0:T(1,128)} %param.11, s32[]{:T(128)} %fusion.195, s32[]{:T(128)S(6)} %mul.107), kind=kLoop, calls=%fused_computation.215 | loop fusion | flops 42 | bytes 108 | tf_op jit(solution)/shard_map/mul | solution.py:97
  12.0 0.6 iota_compare_fusion
  12.6 0.7 broadcast_add_fusion.1
  13.5 2.4 %fusion.16 = f32[1024,256]{1,0:T(8,128)S(1)} fusion(bf16[1,1024,8192]{2,1,0:T(8,128)(2,1)} %param.7, s32[]{:T(128)S(6)} %select_n.178, bf16[1,1024,256]{2,1,0:T(8,128)(2,1)} %param.9), kind=kOutput, calls=%fused_computation.17 | convolution fusion | flops 536870912 | bytes 3670020 | tf_op jit(solution)/shard_map/dot_general | solution.py:18
  16.0 1.6 %collective-permute-start.7 = (bf16[1024,128]{1,0:T(8,128)(2,1)S(1)}, bf16[1024,128]{1,0:T(8,128)(2,1)S(1)}, u32[]{:S(2)}, u32[]{:S(2)}) collective-permute-start(bf16[1024,128]{1,0:T(8,128)(2,1)S(1)} %collective-permute-done), channel_id=1, source_target_pairs={{0,1},{1,0},{2,3},{3,2},{4,5},{5,4},{6,7},{7,6},{8,9},{9,8},{10,11... | collective-permute-start | bytes 786440 | tf_op jit(solution)/shard_map/ppermute | solution.py:58
  17.6 1.6 %collective-permute-start.1 = (bf16[1024,128]{1,0:T(8,128)(2,1)S(1)}, bf16[1024,128]{1,0:T(8,128)(2,1)S(1)}, u32[]{:S(2)}, u32[]{:S(2)}) collective-permute-start(bf16[1024,128]{1,0:T(8,128)(2,1)S(1)} %collective-permute-done), channel_id=1, source_target_pairs={{0,2},{1,3},{2,4},{3,5},{4,6},{5,7},{6,0},{7,1},{8,10},{9,11},{10,... | collective-permute-start | bytes 786440 | tf_op jit(solution)/shard_map/ppermute | solution.py:56
  19.2 1.0 collective-permute-start.8
  20.2 2.8 %fusion.14 = f32[1024,256]{1,0:T(8,128)S(1)} fusion(bf16[1,1024,8192]{2,1,0:T(8,128)(2,1)} %param.7, s32[]{:T(128)S(6)} %select_n.180, bf16[1024,128]{1,0:T(8,128)(2,1)S(1)} %collective-permute-done.2, bf16[1024,128]{1,0:T(8,128)(2,1)S(1)} %collective-permute-done), kind=kOutput, calls=%fused_computation.15 | convolution fusion | flops 537919488 | bytes 3670020 | tf_op jit(solution)/shard_map/dot_general | solution.py:18
  23.2 2.4 %add_add_fusion = f32[1024,256]{1,0:T(8,128)S(1)} fusion(f32[1024,256]{1,0:T(8,128)S(1)} %fusion.16, f32[1024,256]{1,0:T(8,128)S(1)} %fusion.14, bf16[1,1024,8192]{2,1,0:T(8,128)(2,1)} %param.7, s32[]{:T(128)S(6)} %select_n.182, bf16[1024,128]{1,0:T(8,128)(2,1)S(1)} %collective-permute-done.4, bf16[1024,128]{1,0:T(8,128)(2,1)S(1)} %collective-permute-done.3), kind=kOutput, calls=%fused_computation.83 | convolution fusion | flops 538443776 | bytes 5767172 | tf_op jit(solution)/shard_map/dot_general | solution.py:18
  26.1 1.2 %collective-permute-start.5 = (bf16[1024,128]{1,0:T(8,128)(2,1)S(1)}, bf16[1024,128]{1,0:T(8,128)(2,1)S(1)}, u32[]{:S(2)}, u32[]{:S(2)}) collective-permute-start(bf16[1024,128]{1,0:T(8,128)(2,1)S(1)} %collective-permute-done.1), channel_id=1, source_target_pairs={{0,2},{1,3},{2,4},{3,5},{4,6},{5,7},{6,0},{7,1},{8,10},{9,11},{10,... | collective-permute-start | bytes 786440 | tf_op jit(solution)/shard_map/ppermute | solution.py:56
  27.2 1.4 %collective-permute-start.10 = (bf16[1024,128]{1,0:T(8,128)(2,1)S(1)}, bf16[1024,128]{1,0:T(8,128)(2,1)S(1)}, u32[]{:S(2)}, u32[]{:S(2)}) collective-permute-start(bf16[1024,128]{1,0:T(8,128)(2,1)S(1)} %collective-permute-done.1), channel_id=1, source_target_pairs={{0,1},{1,0},{2,3},{3,2},{4,5},{5,4},{6,7},{7,6},{8,9},{9,8},{10,11... | collective-permute-start | bytes 786440 | tf_op jit(solution)/shard_map/ppermute | solution.py:58
  28.6 5.6 %collective-permute-done.6 = bf16[1024,128]{1,0:T(8,128)(2,1)S(1)} collective-permute-done((bf16[1024,128]{1,0:T(8,128)(2,1)S(1)}, bf16[1024,128]{1,0:T(8,128)(2,1)S(1)}, u32[]{:S(2)}, u32[]{:S(2)}) %collective-permute-start.6) | collective-permute-done | bytes 262176 | tf_op jit(solution)/shard_map/ppermute | solution.py:56
  34.2 1.2 %collective-permute-start.11 = (bf16[1024,128]{1,0:T(8,128)(2,1)S(1)}, bf16[1024,128]{1,0:T(8,128)(2,1)S(1)}, u32[]{:S(2)}, u32[]{:S(2)}) collective-permute-start(bf16[1024,128]{1,0:T(8,128)(2,1)S(1)} %collective-permute-done.6), channel_id=1, source_target_pairs={{0,1},{1,0},{2,3},{3,2},{4,5},{5,4},{6,7},{7,6},{8,9},{9,8},{10,11... | collective-permute-start | bytes 786440 | tf_op jit(solution)/shard_map/ppermute | solution.py:58
  35.4 2.3 %fusion.8 = f32[1024,256]{1,0:T(8,128)S(1)} fusion(bf16[1,1024,8192]{2,1,0:T(8,128)(2,1)} %param.7, s32[]{:T(128)S(6)} %select_n.185, bf16[1024,128]{1,0:T(8,128)(2,1)S(1)} %collective-permute-done.8, bf16[1024,128]{1,0:T(8,128)(2,1)S(1)} %collective-permute-done.7), kind=kOutput, calls=%fused_computation.9 | convolution fusion | flops 537919488 | bytes 3670020 | tf_op jit(solution)/shard_map/dot_general | solution.py:18
  37.8 0.7 fusion.57
  38.5 1.3 %collective-permute-done.5 = bf16[1024,128]{1,0:T(8,128)(2,1)S(1)} collective-permute-done((bf16[1024,128]{1,0:T(8,128)(2,1)S(1)}, bf16[1024,128]{1,0:T(8,128)(2,1)S(1)}, u32[]{:S(2)}, u32[]{:S(2)}) %collective-permute-start.5) | collective-permute-done | bytes 262176 | tf_op jit(solution)/shard_map/ppermute | solution.py:56
  39.8 1.2 %collective-permute-start.12 = (bf16[1024,128]{1,0:T(8,128)(2,1)S(1)}, bf16[1024,128]{1,0:T(8,128)(2,1)S(1)}, u32[]{:S(2)}, u32[]{:S(2)}) collective-permute-start(bf16[1024,128]{1,0:T(8,128)(2,1)S(1)} %collective-permute-done.5), channel_id=1, source_target_pairs={{0,1},{1,0},{2,3},{3,2},{4,5},{5,4},{6,7},{7,6},{8,9},{9,8},{10,11... | collective-permute-start | bytes 786440 | tf_op jit(solution)/shard_map/ppermute | solution.py:58
  41.0 2.6 %collective-permute-done.9 = bf16[1024,128]{1,0:T(8,128)(2,1)S(1)} collective-permute-done((bf16[1024,128]{1,0:T(8,128)(2,1)S(1)}, bf16[1024,128]{1,0:T(8,128)(2,1)S(1)}, u32[]{:S(2)}, u32[]{:S(2)}) %collective-permute-start.9) | collective-permute-done | bytes 262176 | tf_op jit(solution)/shard_map/ppermute | solution.py:56
  43.6 0.8 collective-permute-start.13
  44.4 0.7 fusion.4
  45.1 0.7 fusion.63
  45.9 3.1 %collective-permute-done.12 = bf16[1024,128]{1,0:T(8,128)(2,1)S(1)} collective-permute-done((bf16[1024,128]{1,0:T(8,128)(2,1)S(1)}, bf16[1024,128]{1,0:T(8,128)(2,1)S(1)}, u32[]{:S(2)}, u32[]{:S(2)}) %collective-permute-start.12) | collective-permute-done | bytes 262176 | tf_op jit(solution)/shard_map/ppermute | solution.py:58
  49.0 0.7 fusion.104
  50.2 1.7 %collective-permute-done.13 = bf16[1024,128]{1,0:T(8,128)(2,1)S(1)} collective-permute-done((bf16[1024,128]{1,0:T(8,128)(2,1)S(1)}, bf16[1024,128]{1,0:T(8,128)(2,1)S(1)}, u32[]{:S(2)}, u32[]{:S(2)}) %collective-permute-start.13) | collective-permute-done | bytes 262176 | tf_op jit(solution)/shard_map/ppermute | solution.py:58
  51.9 0.7 fusion.81
  52.6 1.6 %collective-permute-start.16 = (bf16[1024,128]{1,0:T(8,128)(2,1)S(1)}, bf16[1024,128]{1,0:T(8,128)(2,1)S(1)}, u32[]{:S(2)}, u32[]{:S(2)}) collective-permute-start(bf16[1024,128]{1,0:T(8,128)(2,1)S(1)} %fusion.81), channel_id=1, source_target_pairs={{0,2},{1,3},{2,4},{3,5},{4,6},{5,7},{6,0},{7,1},{8,10},{9,11},{10,... | collective-permute-start | bytes 786440 | tf_op jit(solution)/shard_map/ppermute | solution.py:56
  54.2 1.5 %collective-permute-start.17 = (bf16[1024,128]{1,0:T(8,128)(2,1)S(1)}, bf16[1024,128]{1,0:T(8,128)(2,1)S(1)}, u32[]{:S(2)}, u32[]{:S(2)}) collective-permute-start(bf16[1024,128]{1,0:T(8,128)(2,1)S(1)} %fusion.104), channel_id=1, source_target_pairs={{0,1},{1,0},{2,3},{3,2},{4,5},{5,4},{6,7},{7,6},{8,9},{9,8},{10,11... | collective-permute-start | bytes 786440 | tf_op jit(solution)/shard_map/ppermute | solution.py:58
  56.2 0.8 fusion.154
  57.1 0.6 fusion.43
  57.7 2.3 %collective-permute-done.14 = bf16[1024,128]{1,0:T(8,128)(2,1)S(1)} collective-permute-done((bf16[1024,128]{1,0:T(8,128)(2,1)S(1)}, bf16[1024,128]{1,0:T(8,128)(2,1)S(1)}, u32[]{:S(2)}, u32[]{:S(2)}) %collective-permute-start.14) | collective-permute-done | bytes 262176 | tf_op jit(solution)/shard_map/ppermute | solution.py:56
  60.0 1.9 %collective-permute-start.21 = (bf16[1024,128]{1,0:T(8,128)(2,1)S(1)}, bf16[1024,128]{1,0:T(8,128)(2,1)S(1)}, u32[]{:S(2)}, u32[]{:S(2)}) collective-permute-start(bf16[1024,128]{1,0:T(8,128)(2,1)S(1)} %collective-permute-done.14), channel_id=1, source_target_pairs={{0,1},{1,0},{2,3},{3,2},{4,5},{5,4},{6,7},{7,6},{8,9},{9,8},{10,11... | collective-permute-start | bytes 786440 | tf_op jit(solution)/shard_map/ppermute | solution.py:58
  61.9 2.6 %collective-permute-done.16 = bf16[1024,128]{1,0:T(8,128)(2,1)S(1)} collective-permute-done((bf16[1024,128]{1,0:T(8,128)(2,1)S(1)}, bf16[1024,128]{1,0:T(8,128)(2,1)S(1)}, u32[]{:S(2)}, u32[]{:S(2)}) %collective-permute-start.16) | collective-permute-done | bytes 262176 | tf_op jit(solution)/shard_map/ppermute | solution.py:56
  64.4 3.0 %collective-permute-start.22 = (bf16[1024,128]{1,0:T(8,128)(2,1)S(1)}, bf16[1024,128]{1,0:T(8,128)(2,1)S(1)}, u32[]{:S(2)}, u32[]{:S(2)}) collective-permute-start(bf16[1024,128]{1,0:T(8,128)(2,1)S(1)} %collective-permute-done.16), channel_id=1, source_target_pairs={{0,1},{1,0},{2,3},{3,2},{4,5},{5,4},{6,7},{7,6},{8,9},{9,8},{10,11... | collective-permute-start | bytes 786440 | tf_op jit(solution)/shard_map/ppermute | solution.py:58
  67.5 0.6 fusion.41
  68.2 0.9 collective-permute-done.18
  69.7 3.1 %collective-permute-done.15 = bf16[1024,128]{1,0:T(8,128)(2,1)S(1)} collective-permute-done((bf16[1024,128]{1,0:T(8,128)(2,1)S(1)}, bf16[1024,128]{1,0:T(8,128)(2,1)S(1)}, u32[]{:S(2)}, u32[]{:S(2)}) %collective-permute-start.15) | collective-permute-done | bytes 262176 | tf_op jit(solution)/shard_map/ppermute | solution.py:56
  73.1 4.9 %collective-permute-done.20 = bf16[1024,128]{1,0:T(8,128)(2,1)S(1)} collective-permute-done((bf16[1024,128]{1,0:T(8,128)(2,1)S(1)}, bf16[1024,128]{1,0:T(8,128)(2,1)S(1)}, u32[]{:S(2)}, u32[]{:S(2)}) %collective-permute-start.20) | collective-permute-done | bytes 262176 | tf_op jit(solution)/shard_map/ppermute | solution.py:56
  78.1 1.1 collective-permute-start.25
  79.2 1.1 collective-permute-done.22
  80.3 0.6 fusion.35
  80.9 0.6 fusion.69
  81.5 1.8 %collective-permute-done.19 = bf16[1024,128]{1,0:T(8,128)(2,1)S(1)} collective-permute-done((bf16[1024,128]{1,0:T(8,128)(2,1)S(1)}, bf16[1024,128]{1,0:T(8,128)(2,1)S(1)}, u32[]{:S(2)}, u32[]{:S(2)}) %collective-permute-start.19) | collective-permute-done | bytes 262176 | tf_op jit(solution)/shard_map/ppermute | solution.py:56
  83.3 1.0 collective-permute-start.26
  84.3 3.1 %collective-permute-done.23 = bf16[1024,128]{1,0:T(8,128)(2,1)S(1)} collective-permute-done((bf16[1024,128]{1,0:T(8,128)(2,1)S(1)}, bf16[1024,128]{1,0:T(8,128)(2,1)S(1)}, u32[]{:S(2)}, u32[]{:S(2)}) %collective-permute-start.23) | collective-permute-done | bytes 262176 | tf_op jit(solution)/shard_map/ppermute | solution.py:56
  87.4 0.9 collective-permute-start.30
  88.3 3.3 %collective-permute-done.25 = bf16[1024,128]{1,0:T(8,128)(2,1)S(1)} collective-permute-done((bf16[1024,128]{1,0:T(8,128)(2,1)S(1)}, bf16[1024,128]{1,0:T(8,128)(2,1)S(1)}, u32[]{:S(2)}, u32[]{:S(2)}) %collective-permute-start.25) | collective-permute-done | bytes 262176 | tf_op jit(solution)/shard_map/ppermute | solution.py:58
  91.6 0.6 fusion.31
  92.1 0.6 fusion.75
  92.7 4.4 %collective-permute-done.26 = bf16[1024,128]{1,0:T(8,128)(2,1)S(1)} collective-permute-done((bf16[1024,128]{1,0:T(8,128)(2,1)S(1)}, bf16[1024,128]{1,0:T(8,128)(2,1)S(1)}, u32[]{:S(2)}, u32[]{:S(2)}) %collective-permute-start.26) | collective-permute-done | bytes 262176 | tf_op jit(solution)/shard_map/ppermute | solution.py:58
  98.6 1.4 %collective-permute-done.30 = bf16[1024,128]{1,0:T(8,128)(2,1)S(1)} collective-permute-done((bf16[1024,128]{1,0:T(8,128)(2,1)S(1)}, bf16[1024,128]{1,0:T(8,128)(2,1)S(1)}, u32[]{:S(2)}, u32[]{:S(2)}) %collective-permute-start.30) | collective-permute-done | bytes 262176 | tf_op jit(solution)/shard_map/ppermute | solution.py:58
  101.8 0.6 convolution_subtract_fusion.1
  102.7 1.6 %collective-permute-start.28 = (bf16[272,128]{1,0:T(8,128)(2,1)S(1)}, bf16[272,128]{1,0:T(8,128)(2,1)S(1)}, u32[]{:S(2)}, u32[]{:S(2)}) collective-permute-start(bf16[272,128]{1,0:T(8,128)(2,1)S(1)} %pad_maximum_fusion.3), channel_id=1, source_target_pairs={{0,16},{8,24},{16,0},{24,8},{1,17},{9,25},{17,1},{25,9},{2,18},{10... | collective-permute-start | bytes 208904 | tf_op jit(solution)/shard_map/ppermute | solution.py:116
  104.2 0.6 collective-permute-start.27
  104.9 1.5 %collective-permute-start.32 = (bf16[256,128]{1,0:T(8,128)(2,1)S(1)}, bf16[256,128]{1,0:T(8,128)(2,1)S(1)}, u32[]{:S(2)}, u32[]{:S(2)}) collective-permute-start(bf16[256,128]{1,0:T(8,128)(2,1)S(1)} %convolution_convert_fusion.1), channel_id=1, source_target_pairs={{0,16},{8,24},{16,0},{24,8},{1,17},{9,25},{17,1},{25,9},{2,18},{10... | collective-permute-start | bytes 196616 | tf_op jit(solution)/shard_map/ppermute | solution.py:116
  106.4 0.7 collective-permute-done.28
  107.0 1.5 %collective-permute-done.29 = bf16[272,128]{1,0:T(8,128)(2,1)S(1)} collective-permute-done((bf16[272,128]{1,0:T(8,128)(2,1)S(1)}, bf16[272,128]{1,0:T(8,128)(2,1)S(1)}, u32[]{:S(2)}, u32[]{:S(2)}) %collective-permute-start.29) | collective-permute-done | bytes 69664 | tf_op jit(solution)/shard_map/ppermute | solution.py:116
  110.1 1.2 %collective-permute-done.33 = bf16[256,128]{1,0:T(8,128)(2,1)S(1)} collective-permute-done((bf16[256,128]{1,0:T(8,128)(2,1)S(1)}, bf16[256,128]{1,0:T(8,128)(2,1)S(1)}, u32[]{:S(2)}, u32[]{:S(2)}) %collective-permute-start.33) | collective-permute-done | bytes 65568 | tf_op jit(solution)/shard_map/ppermute | solution.py:116
  111.8 0.8 maximum_bitcast_fusion
  (74 shorter events, 8.7 us)
Async XLA Ops:
  1.7 14.3 %collective-permute-start = (bf16[1024,128]{1,0:T(8,128)(2,1)S(1)}, bf16[1024,128]{1,0:T(8,128)(2,1)S(1)}, u32[]{:S(2)}, u32[]{:S(2)}) collective-permute-start(bf16[1024,128]{1,0:T(8,128)(2,1)S(1)} %get-tuple-element.28), channel_id=1, source_target_pairs={{0,2},{1,3},{2,4},{3,5},{4,6},{5,7},{6,0},{7,1},{8,10},{9,11},{10,... | collective-permute-start | bytes 786440 | tf_op jit(solution)/shard_map/ppermute | solution.py:56
  4.8 18.3 %collective-permute-start.3 = (bf16[1024,128]{1,0:T(8,128)(2,1)S(1)}, bf16[1024,128]{1,0:T(8,128)(2,1)S(1)}, u32[]{:S(2)}, u32[]{:S(2)}) collective-permute-start(bf16[1024,128]{1,0:T(8,128)(2,1)S(1)} %get-tuple-element.28), channel_id=1, source_target_pairs={{0,1},{1,0},{2,3},{3,2},{4,5},{5,4},{6,7},{7,6},{8,9},{9,8},{10,11... | collective-permute-start | bytes 786440 | tf_op jit(solution)/shard_map/ppermute | solution.py:58
  6.3 12.9 %collective-permute-start.2 = (bf16[1024,128]{1,0:T(8,128)(2,1)S(1)}, bf16[1024,128]{1,0:T(8,128)(2,1)S(1)}, u32[]{:S(2)}, u32[]{:S(2)}) collective-permute-start(bf16[1024,128]{1,0:T(8,128)(2,1)S(1)} %get-tuple-element.29), channel_id=1, source_target_pairs={{0,2},{1,3},{2,4},{3,5},{4,6},{5,7},{6,0},{7,1},{8,10},{9,11},{10,... | collective-permute-start | bytes 786440 | tf_op jit(solution)/shard_map/ppermute | solution.py:56
  7.9 15.3 %collective-permute-start.4 = (bf16[1024,128]{1,0:T(8,128)(2,1)S(1)}, bf16[1024,128]{1,0:T(8,128)(2,1)S(1)}, u32[]{:S(2)}, u32[]{:S(2)}) collective-permute-start(bf16[1024,128]{1,0:T(8,128)(2,1)S(1)} %get-tuple-element.29), channel_id=1, source_target_pairs={{0,1},{1,0},{2,3},{3,2},{4,5},{5,4},{6,7},{7,6},{8,9},{9,8},{10,11... | collective-permute-start | bytes 786440 | tf_op jit(solution)/shard_map/ppermute | solution.py:58
  16.0 21.7 %copy-start = (bf16[1,1024,8192]{2,1,0:T(8,128)(2,1)S(1)}, bf16[1,1024,8192]{2,1,0:T(8,128)(2,1)}, u32[]{:S(2)}) copy-start(bf16[1,1024,8192]{2,1,0:T(8,128)(2,1)} %param.7) | copy-start | bytes 50331652
  16.0 19.4 %collective-permute-start.7 = (bf16[1024,128]{1,0:T(8,128)(2,1)S(1)}, bf16[1024,128]{1,0:T(8,128)(2,1)S(1)}, u32[]{:S(2)}, u32[]{:S(2)}) collective-permute-start(bf16[1024,128]{1,0:T(8,128)(2,1)S(1)} %collective-permute-done), channel_id=1, source_target_pairs={{0,1},{1,0},{2,3},{3,2},{4,5},{5,4},{6,7},{7,6},{8,9},{9,8},{10,11... | collective-permute-start | bytes 786440 | tf_op jit(solution)/shard_map/ppermute | solution.py:58
  17.6 8.4 %collective-permute-start.1 = (bf16[1024,128]{1,0:T(8,128)(2,1)S(1)}, bf16[1024,128]{1,0:T(8,128)(2,1)S(1)}, u32[]{:S(2)}, u32[]{:S(2)}) collective-permute-start(bf16[1024,128]{1,0:T(8,128)(2,1)S(1)} %collective-permute-done), channel_id=1, source_target_pairs={{0,2},{1,3},{2,4},{3,5},{4,6},{5,7},{6,0},{7,1},{8,10},{9,11},{10,... | collective-permute-start | bytes 786440 | tf_op jit(solution)/shard_map/ppermute | solution.py:56
  19.2 16.2 %collective-permute-start.8 = (bf16[1024,128]{1,0:T(8,128)(2,1)S(1)}, bf16[1024,128]{1,0:T(8,128)(2,1)S(1)}, u32[]{:S(2)}, u32[]{:S(2)}) collective-permute-start(bf16[1024,128]{1,0:T(8,128)(2,1)S(1)} %collective-permute-done.2), channel_id=1, source_target_pairs={{0,1},{1,0},{2,3},{3,2},{4,5},{5,4},{6,7},{7,6},{8,9},{9,8},{10,11... | collective-permute-start | bytes 786440 | tf_op jit(solution)/shard_map/ppermute | solution.py:58
  23.1 11.1 %collective-permute-start.6 = (bf16[1024,128]{1,0:T(8,128)(2,1)S(1)}, bf16[1024,128]{1,0:T(8,128)(2,1)S(1)}, u32[]{:S(2)}, u32[]{:S(2)}) collective-permute-start(bf16[1024,128]{1,0:T(8,128)(2,1)S(1)} %collective-permute-done.2), channel_id=1, source_target_pairs={{0,2},{1,3},{2,4},{3,5},{4,6},{5,7},{6,0},{7,1},{8,10},{9,11},{10,... | collective-permute-start | bytes 786440 | tf_op jit(solution)/shard_map/ppermute | solution.py:56
  26.1 13.7 %collective-permute-start.5 = (bf16[1024,128]{1,0:T(8,128)(2,1)S(1)}, bf16[1024,128]{1,0:T(8,128)(2,1)S(1)}, u32[]{:S(2)}, u32[]{:S(2)}) collective-permute-start(bf16[1024,128]{1,0:T(8,128)(2,1)S(1)} %collective-permute-done.1), channel_id=1, source_target_pairs={{0,2},{1,3},{2,4},{3,5},{4,6},{5,7},{6,0},{7,1},{8,10},{9,11},{10,... | collective-permute-start | bytes 786440 | tf_op jit(solution)/shard_map/ppermute | solution.py:56
  27.2 17.2 %collective-permute-start.10 = (bf16[1024,128]{1,0:T(8,128)(2,1)S(1)}, bf16[1024,128]{1,0:T(8,128)(2,1)S(1)}, u32[]{:S(2)}, u32[]{:S(2)}) collective-permute-start(bf16[1024,128]{1,0:T(8,128)(2,1)S(1)} %collective-permute-done.1), channel_id=1, source_target_pairs={{0,1},{1,0},{2,3},{3,2},{4,5},{5,4},{6,7},{7,6},{8,9},{9,8},{10,11... | collective-permute-start | bytes 786440 | tf_op jit(solution)/shard_map/ppermute | solution.py:58
  34.2 10.2 %collective-permute-start.11 = (bf16[1024,128]{1,0:T(8,128)(2,1)S(1)}, bf16[1024,128]{1,0:T(8,128)(2,1)S(1)}, u32[]{:S(2)}, u32[]{:S(2)}) collective-permute-start(bf16[1024,128]{1,0:T(8,128)(2,1)S(1)} %collective-permute-done.6), channel_id=1, source_target_pairs={{0,1},{1,0},{2,3},{3,2},{4,5},{5,4},{6,7},{7,6},{8,9},{9,8},{10,11... | collective-permute-start | bytes 786440 | tf_op jit(solution)/shard_map/ppermute | solution.py:58
  35.4 8.2 %collective-permute-start.9 = (bf16[1024,128]{1,0:T(8,128)(2,1)S(1)}, bf16[1024,128]{1,0:T(8,128)(2,1)S(1)}, u32[]{:S(2)}, u32[]{:S(2)}) collective-permute-start(bf16[1024,128]{1,0:T(8,128)(2,1)S(1)} %collective-permute-done.6), channel_id=1, source_target_pairs={{0,2},{1,3},{2,4},{3,5},{4,6},{5,7},{6,0},{7,1},{8,10},{9,11},{10,... | collective-permute-start | bytes 786440 | tf_op jit(solution)/shard_map/ppermute | solution.py:56
  37.8 19.4 %slice-start = ((s8[12582912]{0:T(1024)(128)(4,1)}), s8[4194304]{0:T(1024)(128)(4,1)S(1)}, s32[]{:S(2)}) async-start(s8[12582912]{0:T(1024)(128)(4,1)} %bitcast.137), calls=%async_computation | async-start | bytes 8388608
  38.5 18.6 %slice-start.1 = ((s8[12582912]{0:T(1024)(128)(4,1)}), s8[4194304]{0:T(1024)(128)(4,1)S(1)}, s32[]{:S(2)}) async-start(s8[12582912]{0:T(1024)(128)(4,1)} %bitcast.137), calls=%async_computation.1 | async-start | bytes 8388608
  39.8 9.2 %collective-permute-start.12 = (bf16[1024,128]{1,0:T(8,128)(2,1)S(1)}, bf16[1024,128]{1,0:T(8,128)(2,1)S(1)}, u32[]{:S(2)}, u32[]{:S(2)}) collective-permute-start(bf16[1024,128]{1,0:T(8,128)(2,1)S(1)} %collective-permute-done.5), channel_id=1, source_target_pairs={{0,1},{1,0},{2,3},{3,2},{4,5},{5,4},{6,7},{7,6},{8,9},{9,8},{10,11... | collective-permute-start | bytes 786440 | tf_op jit(solution)/shard_map/ppermute | solution.py:58
  43.6 8.3 %collective-permute-start.13 = (bf16[1024,128]{1,0:T(8,128)(2,1)S(1)}, bf16[1024,128]{1,0:T(8,128)(2,1)S(1)}, u32[]{:S(2)}, u32[]{:S(2)}) collective-permute-start(bf16[1024,128]{1,0:T(8,128)(2,1)S(1)} %collective-permute-done.9), channel_id=1, source_target_pairs={{0,1},{1,0},{2,3},{3,2},{4,5},{5,4},{6,7},{7,6},{8,9},{9,8},{10,11... | collective-permute-start | bytes 786440 | tf_op jit(solution)/shard_map/ppermute | solution.py:58
  45.1 12.0 %slice-start.2 = ((s8[12582912]{0:T(1024)(128)(4,1)}), s8[4194304]{0:T(1024)(128)(4,1)S(1)}, s32[]{:S(2)}) async-start(s8[12582912]{0:T(1024)(128)(4,1)} %bitcast.137), calls=%async_computation.2 | async-start | bytes 8388608
  49.7 10.3 %collective-permute-start.14 = (bf16[1024,128]{1,0:T(8,128)(2,1)S(1)}, bf16[1024,128]{1,0:T(8,128)(2,1)S(1)}, u32[]{:S(2)}, u32[]{:S(2)}) collective-permute-start(bf16[1024,128]{1,0:T(8,128)(2,1)S(1)} %fusion.104), channel_id=1, source_target_pairs={{0,2},{1,3},{2,4},{3,5},{4,6},{5,7},{6,0},{7,1},{8,10},{9,11},{10,... | collective-permute-start | bytes 786440 | tf_op jit(solution)/shard_map/ppermute | solution.py:56
  52.6 11.9 %collective-permute-start.16 = (bf16[1024,128]{1,0:T(8,128)(2,1)S(1)}, bf16[1024,128]{1,0:T(8,128)(2,1)S(1)}, u32[]{:S(2)}, u32[]{:S(2)}) collective-permute-start(bf16[1024,128]{1,0:T(8,128)(2,1)S(1)} %fusion.81), channel_id=1, source_target_pairs={{0,2},{1,3},{2,4},{3,5},{4,6},{5,7},{6,0},{7,1},{8,10},{9,11},{10,... | collective-permute-start | bytes 786440 | tf_op jit(solution)/shard_map/ppermute | solution.py:56
  54.2 13.9 %collective-permute-start.17 = (bf16[1024,128]{1,0:T(8,128)(2,1)S(1)}, bf16[1024,128]{1,0:T(8,128)(2,1)S(1)}, u32[]{:S(2)}, u32[]{:S(2)}) collective-permute-start(bf16[1024,128]{1,0:T(8,128)(2,1)S(1)} %fusion.104), channel_id=1, source_target_pairs={{0,1},{1,0},{2,3},{3,2},{4,5},{5,4},{6,7},{7,6},{8,9},{9,8},{10,11... | collective-permute-start | bytes 786440 | tf_op jit(solution)/shard_map/ppermute | solution.py:58
  55.7 13.3 %collective-permute-start.18 = (bf16[1024,128]{1,0:T(8,128)(2,1)S(1)}, bf16[1024,128]{1,0:T(8,128)(2,1)S(1)}, u32[]{:S(2)}, u32[]{:S(2)}) collective-permute-start(bf16[1024,128]{1,0:T(8,128)(2,1)S(1)} %fusion.81), channel_id=1, source_target_pairs={{0,1},{1,0},{2,3},{3,2},{4,5},{5,4},{6,7},{7,6},{8,9},{9,8},{10,11... | collective-permute-start | bytes 786440 | tf_op jit(solution)/shard_map/ppermute | solution.py:58
  60.0 19.2 %collective-permute-start.21 = (bf16[1024,128]{1,0:T(8,128)(2,1)S(1)}, bf16[1024,128]{1,0:T(8,128)(2,1)S(1)}, u32[]{:S(2)}, u32[]{:S(2)}) collective-permute-start(bf16[1024,128]{1,0:T(8,128)(2,1)S(1)} %collective-permute-done.14), channel_id=1, source_target_pairs={{0,1},{1,0},{2,3},{3,2},{4,5},{5,4},{6,7},{7,6},{8,9},{9,8},{10,11... | collective-permute-start | bytes 786440 | tf_op jit(solution)/shard_map/ppermute | solution.py:58
  61.9 10.9 %collective-permute-start.15 = (bf16[1024,128]{1,0:T(8,128)(2,1)S(1)}, bf16[1024,128]{1,0:T(8,128)(2,1)S(1)}, u32[]{:S(2)}, u32[]{:S(2)}) collective-permute-start(bf16[1024,128]{1,0:T(8,128)(2,1)S(1)} %collective-permute-done.14), channel_id=1, source_target_pairs={{0,2},{1,3},{2,4},{3,5},{4,6},{5,7},{6,0},{7,1},{8,10},{9,11},{10,... | collective-permute-start | bytes 786440 | tf_op jit(solution)/shard_map/ppermute | solution.py:56
  64.4 15.9 %collective-permute-start.22 = (bf16[1024,128]{1,0:T(8,128)(2,1)S(1)}, bf16[1024,128]{1,0:T(8,128)(2,1)S(1)}, u32[]{:S(2)}, u32[]{:S(2)}) collective-permute-start(bf16[1024,128]{1,0:T(8,128)(2,1)S(1)} %collective-permute-done.16), channel_id=1, source_target_pairs={{0,1},{1,0},{2,3},{3,2},{4,5},{5,4},{6,7},{7,6},{8,9},{9,8},{10,11... | collective-permute-start | bytes 786440 | tf_op jit(solution)/shard_map/ppermute | solution.py:58
  68.1 10.0 %collective-permute-start.20 = (bf16[1024,128]{1,0:T(8,128)(2,1)S(1)}, bf16[1024,128]{1,0:T(8,128)(2,1)S(1)}, u32[]{:S(2)}, u32[]{:S(2)}) collective-permute-start(bf16[1024,128]{1,0:T(8,128)(2,1)S(1)} %collective-permute-done.16), channel_id=1, source_target_pairs={{0,2},{1,3},{2,4},{3,5},{4,6},{5,7},{6,0},{7,1},{8,10},{9,11},{10,... | collective-permute-start | bytes 786440 | tf_op jit(solution)/shard_map/ppermute | solution.py:56
  69.7 31.5 %copy-start.1 = (bf16[1,512,256]{2,1,0:T(8,128)(2,1)S(1)}, bf16[1,512,256]{2,1,0:T(8,128)(2,1)}, u32[]{:S(2)}) copy-start(bf16[1,512,256]{2,1,0:T(8,128)(2,1)} %param.13) | copy-start | bytes 786436
  72.8 10.4 %collective-permute-start.19 = (bf16[1024,128]{1,0:T(8,128)(2,1)S(1)}, bf16[1024,128]{1,0:T(8,128)(2,1)S(1)}, u32[]{:S(2)}, u32[]{:S(2)}) collective-permute-start(bf16[1024,128]{1,0:T(8,128)(2,1)S(1)} %collective-permute-done.15), channel_id=1, source_target_pairs={{0,2},{1,3},{2,4},{3,5},{4,6},{5,7},{6,0},{7,1},{8,10},{9,11},{10,... | collective-permute-start | bytes 786440 | tf_op jit(solution)/shard_map/ppermute | solution.py:56
  72.8 15.4 %collective-permute-start.24 = (bf16[1024,128]{1,0:T(8,128)(2,1)S(1)}, bf16[1024,128]{1,0:T(8,128)(2,1)S(1)}, u32[]{:S(2)}, u32[]{:S(2)}) collective-permute-start(bf16[1024,128]{1,0:T(8,128)(2,1)S(1)} %collective-permute-done.15), channel_id=1, source_target_pairs={{0,1},{1,0},{2,3},{3,2},{4,5},{5,4},{6,7},{7,6},{8,9},{9,8},{10,11... | collective-permute-start | bytes 786440 | tf_op jit(solution)/shard_map/ppermute | solution.py:58
  78.1 13.5 %collective-permute-start.25 = (bf16[1024,128]{1,0:T(8,128)(2,1)S(1)}, bf16[1024,128]{1,0:T(8,128)(2,1)S(1)}, u32[]{:S(2)}, u32[]{:S(2)}) collective-permute-start(bf16[1024,128]{1,0:T(8,128)(2,1)S(1)} %collective-permute-done.20), channel_id=1, source_target_pairs={{0,1},{1,0},{2,3},{3,2},{4,5},{5,4},{6,7},{7,6},{8,9},{9,8},{10,11... | collective-permute-start | bytes 786440 | tf_op jit(solution)/shard_map/ppermute | solution.py:58
  79.2 8.2 %collective-permute-start.23 = (bf16[1024,128]{1,0:T(8,128)(2,1)S(1)}, bf16[1024,128]{1,0:T(8,128)(2,1)S(1)}, u32[]{:S(2)}, u32[]{:S(2)}) collective-permute-start(bf16[1024,128]{1,0:T(8,128)(2,1)S(1)} %collective-permute-done.20), channel_id=1, source_target_pairs={{0,2},{1,3},{2,4},{3,5},{4,6},{5,7},{6,0},{7,1},{8,10},{9,11},{10,... | collective-permute-start | bytes 786440 | tf_op jit(solution)/shard_map/ppermute | solution.py:56
  83.3 13.9 %collective-permute-start.26 = (bf16[1024,128]{1,0:T(8,128)(2,1)S(1)}, bf16[1024,128]{1,0:T(8,128)(2,1)S(1)}, u32[]{:S(2)}, u32[]{:S(2)}) collective-permute-start(bf16[1024,128]{1,0:T(8,128)(2,1)S(1)} %collective-permute-done.19), channel_id=1, source_target_pairs={{0,1},{1,0},{2,3},{3,2},{4,5},{5,4},{6,7},{7,6},{8,9},{9,8},{10,11... | collective-permute-start | bytes 786440 | tf_op jit(solution)/shard_map/ppermute | solution.py:58
  87.4 12.7 %collective-permute-start.30 = (bf16[1024,128]{1,0:T(8,128)(2,1)S(1)}, bf16[1024,128]{1,0:T(8,128)(2,1)S(1)}, u32[]{:S(2)}, u32[]{:S(2)}) collective-permute-start(bf16[1024,128]{1,0:T(8,128)(2,1)S(1)} %collective-permute-done.23), channel_id=1, source_target_pairs={{0,1},{1,0},{2,3},{3,2},{4,5},{5,4},{6,7},{7,6},{8,9},{9,8},{10,11... | collective-permute-start | bytes 786440 | tf_op jit(solution)/shard_map/ppermute | solution.py:58
  102.7 4.4 %collective-permute-start.28 = (bf16[272,128]{1,0:T(8,128)(2,1)S(1)}, bf16[272,128]{1,0:T(8,128)(2,1)S(1)}, u32[]{:S(2)}, u32[]{:S(2)}) collective-permute-start(bf16[272,128]{1,0:T(8,128)(2,1)S(1)} %pad_maximum_fusion.3), channel_id=1, source_target_pairs={{0,16},{8,24},{16,0},{24,8},{1,17},{9,25},{17,1},{25,9},{2,18},{10... | collective-permute-start | bytes 208904 | tf_op jit(solution)/shard_map/ppermute | solution.py:116
  104.2 4.4 %collective-permute-start.29 = (bf16[272,128]{1,0:T(8,128)(2,1)S(1)}, bf16[272,128]{1,0:T(8,128)(2,1)S(1)}, u32[]{:S(2)}, u32[]{:S(2)}) collective-permute-start(bf16[272,128]{1,0:T(8,128)(2,1)S(1)} %pad_maximum_fusion.4), channel_id=1, source_target_pairs={{0,24},{8,16},{16,8},{24,0},{1,25},{9,17},{17,9},{25,1},{2,26},{10... | collective-permute-start | bytes 208904 | tf_op jit(solution)/shard_map/ppermute | solution.py:116
  104.2 4.3 %collective-permute-start.27 = (bf16[272,128]{1,0:T(8,128)(2,1)S(1)}, bf16[272,128]{1,0:T(8,128)(2,1)S(1)}, u32[]{:S(2)}, u32[]{:S(2)}) collective-permute-start(bf16[272,128]{1,0:T(8,128)(2,1)S(1)} %pad_maximum_fusion.2), channel_id=1, source_target_pairs={{0,8},{8,0},{16,24},{24,16},{1,9},{9,1},{17,25},{25,17},{2,10},{10... | collective-permute-start | bytes 208904 | tf_op jit(solution)/shard_map/ppermute | solution.py:116
  104.9 5.0 %collective-permute-start.32 = (bf16[256,128]{1,0:T(8,128)(2,1)S(1)}, bf16[256,128]{1,0:T(8,128)(2,1)S(1)}, u32[]{:S(2)}, u32[]{:S(2)}) collective-permute-start(bf16[256,128]{1,0:T(8,128)(2,1)S(1)} %convolution_convert_fusion.1), channel_id=1, source_target_pairs={{0,16},{8,24},{16,0},{24,8},{1,17},{9,25},{17,1},{25,9},{2,18},{10... | collective-permute-start | bytes 196616 | tf_op jit(solution)/shard_map/ppermute | solution.py:116
  106.4 5.0 %collective-permute-start.33 = (bf16[256,128]{1,0:T(8,128)(2,1)S(1)}, bf16[256,128]{1,0:T(8,128)(2,1)S(1)}, u32[]{:S(2)}, u32[]{:S(2)}) collective-permute-start(bf16[256,128]{1,0:T(8,128)(2,1)S(1)} %convolution_convert_fusion), channel_id=1, source_target_pairs={{0,24},{8,16},{16,8},{24,0},{1,25},{9,17},{17,9},{25,1},{2,26},{10... | collective-permute-start | bytes 196616 | tf_op jit(solution)/shard_map/ppermute | solution.py:116
  107.0 4.5 %collective-permute-start.31 = (bf16[256,128]{1,0:T(8,128)(2,1)S(1)}, bf16[256,128]{1,0:T(8,128)(2,1)S(1)}, u32[]{:S(2)}, u32[]{:S(2)}) collective-permute-start(bf16[256,128]{1,0:T(8,128)(2,1)S(1)} %convolution_convert_fusion.2), channel_id=1, source_target_pairs={{0,8},{8,0},{16,24},{24,16},{1,9},{9,1},{17,25},{25,17},{2,10},{10... | collective-permute-start | bytes 196616 | tf_op jit(solution)/shard_map/ppermute | solution.py:116
where the time goes:
time: 113 us
  waiting for transfers between devices  47.8 us (42%)
  starting transfers between devices  32.8 us (29%)
  matrix products  23 us (20%)
  other arithmetic  6.81 us (6%)
  between operations  1.19 us (1%)
    ppermute x12, waiting for transfers between devices, gathered_product(): lax.ppermute(b, 'wide', z_ring)  27.8 us
    dot_general x32, matrix products, dot(): return row_major(jnp.dot(a, b, preferred_element_type=jnp.float32))  23 us
    ppermute x16, starting transfers between devices, gathered_product(): lax.ppermute(b, 'wide', y_shifts[shift])  19.5 us
    ppermute x16, waiting for transfers between devices, gathered_product(): lax.ppermute(b, 'wide', y_shifts[shift])  16 us
    ppermute x12, starting transfers between devices, gathered_product(): lax.ppermute(b, 'wide', z_ring)  9.58 us
    ppermute x6, waiting for transfers between devices, body(): values = lax.ppermute(values, 'front', swaps[delta])  3.94 us
    ppermute x6, starting transfers between devices, body(): values = lax.ppermute(values, 'front', swaps[delta])  3.69 us
  transfers between devices with their start and end apart: 34, of which 21 were waited for; matrix products, arithmetic and copies ran while one was open for 23% of the time, Pallas kernels for 0%

commit v1 on v0

--- a/solution.py
+++ b/solution.py
@@ -44,7 +44,7 @@
         columns = lax.dynamic_slice_in_dim(matrix, block_of(step, shift) * rows, rows, 1)
         return dot(columns, values)
 
-    def gathered_product(matrix, blocks):
+    def gathered_product(matrix, blocks, paired):
         column_count = len(blocks)
         total = part(matrix, 0, 0, jnp.concatenate(blocks, axis=1))
         waiting = []
@@ -53,6 +53,11 @@
             held_now = following
             if step:
                 held_now[0], total = lax.optimization_barrier((held_now[0], total))
+                for column in paired[step]:
+                    last = [pieces[column] for _, _, pieces in waiting]
+                    held_now[column], last = lax.optimization_barrier((held_now[column], last))
+                    for entry, piece in zip(waiting, last):
+                        entry[2][column] = piece
             following = [lax.ppermute(b, "wide", z_ring) for b in held_now] if step < depth - 1 else None
             passed = [
                 [lax.ppermute(b, "wide", y_shifts[shift]) for b in held_now]
@@ -99,10 +104,10 @@
     picker = picker.reshape(fronts, CAPACITY * height, tiles * height)
 
     cuts = range(0, width, LANES)
-    solved = gathered_product(inv_diag[0], [rhs[0][:, c:c + LANES] for c in cuts])
+    solved = gathered_product(inv_diag[0], [rhs[0][:, c:c + LANES] for c in cuts], ((), (0, 1), (0, 1), ()))
     numbers = jnp.arange(parent_height, dtype=jnp.int32)[:, None]
 
-    updates = gathered_product(below[0], solved)
+    updates = gathered_product(below[0], solved, ((), (0, 1), (0, 1), (0,)))
     tall = CAPACITY * height
     hits = [None] * fronts
     results = []

time: 113 us -> 110 us (0.973)
  waiting for transfers between devices: 47.8 us -> 38.8 us
  starting transfers between devices: 32.8 us -> 39.7 us
    ppermute x12, waiting for transfers between devices: 27.8 us -> 21.2 us  [gathered_product(): lax.ppermute(b, 'wide', z_ring)]
    ppermute x16, starting transfers between devices: 19.5 us -> 23.2 us  [gathered_product(): lax.ppermute(b, 'wide', y_shifts[shift])]
    ppermute x12, starting transfers between devices: 9.58 us -> 12.8 us  [gathered_product(): lax.ppermute(b, 'wide', z_ring)]
    ppermute x16, waiting for transfers between devices: 16 us -> 13.6 us  [gathered_product(): lax.ppermute(b, 'wide', y_shifts[shift])]
  transfers between devices with their start and end apart: 34 -> 34, of which waited for: 21 -> 18; matrix products, arithmetic and copies ran while one was open for 23% -> 23% of each run, Pallas kernels for 0% -> 0%
where the time goes in v1:
time: 110 us
  starting transfers between devices  39.7 us (36%)
  waiting for transfers between devices  38.8 us (35%)
  matrix products  22.4 us (20%)
  other arithmetic  6.81 us (6%)
  local copies, waits for them, and re-layouts  1.11 us (1%)
    ppermute x16, starting transfers between devices, gathered_product(): lax.ppermute(b, 'wide', y_shifts[shift])  23.2 us
    dot_general x32, matrix products, dot(): return row_major(jnp.dot(a, b, preferred_element_type=jnp.float32))  22.4 us
    ppermute x12, waiting for transfers between devices, gathered_product(): lax.ppermute(b, 'wide', z_ring)  21.2 us
    ppermute x16, waiting for transfers between devices, gathered_product(): lax.ppermute(b, 'wide', y_shifts[shift])  13.6 us
    ppermute x12, starting transfers between devices, gathered_product(): lax.ppermute(b, 'wide', z_ring)  12.8 us
    ppermute x6, waiting for transfers between devices, body(): values = lax.ppermute(values, 'front', swaps[delta])  3.94 us
    ppermute x6, starting transfers between devices, body(): values = lax.ppermute(values, 'front', swaps[delta])  3.69 us
  transfers between devices with their start and end apart: 34, of which 18 were waited for; matrix products, arithmetic and copies ran while one was open for 23% of the time, Pallas kernels for 0%

profile of v1, /device:TPU:0, one launch (start us, length us, event | category | flops | bytes accessed | tf_op | source)
XLA Modules:
  0.0 109.9 jit_solution(2075235211084879392)
XLA Ops:
  0.6 1.1 fusion.202
  1.7 3.1 %collective-permute-start = (bf16[1024,128]{1,0:T(8,128)(2,1)S(1)}, bf16[1024,128]{1,0:T(8,128)(2,1)S(1)}, u32[]{:S(2)}, u32[]{:S(2)}) collective-permute-start(bf16[1024,128]{1,0:T(8,128)(2,1)S(1)} %get-tuple-element.64), channel_id=1, source_target_pairs={{0,2},{1,3},{2,4},{3,5},{4,6},{5,7},{6,0},{7,1},{8,10},{9,11},{10,... | collective-permute-start | bytes 786440 | tf_op jit(solution)/shard_map/ppermute | solution.py:61
  4.8 1.5 %collective-permute-start.1 = (bf16[1024,128]{1,0:T(8,128)(2,1)S(1)}, bf16[1024,128]{1,0:T(8,128)(2,1)S(1)}, u32[]{:S(2)}, u32[]{:S(2)}) collective-permute-start(bf16[1024,128]{1,0:T(8,128)(2,1)S(1)} %get-tuple-element.64), channel_id=1, source_target_pairs={{0,1},{1,0},{2,3},{3,2},{4,5},{5,4},{6,7},{7,6},{8,9},{9,8},{10,11... | collective-permute-start | bytes 786440 | tf_op jit(solution)/shard_map/ppermute | solution.py:63
  6.3 1.6 %collective-permute-start.3 = (bf16[1024,128]{1,0:T(8,128)(2,1)S(1)}, bf16[1024,128]{1,0:T(8,128)(2,1)S(1)}, u32[]{:S(2)}, u32[]{:S(2)}) collective-permute-start(bf16[1024,128]{1,0:T(8,128)(2,1)S(1)} %get-tuple-element.65), channel_id=1, source_target_pairs={{0,2},{1,3},{2,4},{3,5},{4,6},{5,7},{6,0},{7,1},{8,10},{9,11},{10,... | collective-permute-start | bytes 786440 | tf_op jit(solution)/shard_map/ppermute | solution.py:61
  8.4 0.9 convert_reduce_fusion
  9.3 1.3 %fusion.187 = s32[]{:T(128)} fusion(s32[4]{0:T(128)} %param.10, s32[]{:T(128)S(6)} %axis_index.25), kind=kLoop, calls=%fused_computation.210 | loop fusion | flops 11 | bytes 24 | tf_op jit(solution)/shard_map/reduce_sum | solution.py:81
  10.6 1.3 %broadcast_multiply_fusion = (s32[6]{0:T(128)S(1)}, s32[6]{0:T(128)S(1)}) fusion(s32[6]{0:T(128)S(1)} %convert_reduce_fusion, s32[]{:T(128)S(6)} %axis_index.25, s32[1,6,1]{1,2,0:T(1,128)} %param.11, s32[]{:T(128)} %fusion.187, s32[]{:T(128)S(6)} %mul.107), kind=kLoop, calls=%fused_computation.211 | loop fusion | flops 42 | bytes 108 | tf_op jit(solution)/shard_map/mul | solution.py:102
  12.0 0.7 broadcast_add_fusion.1
  12.9 2.4 %fusion.16 = f32[1024,256]{1,0:T(8,128)S(1)} fusion(bf16[1,1024,8192]{2,1,0:T(8,128)(2,1)} %param.7, s32[]{:T(128)S(6)} %select_n.178, bf16[1,1024,256]{2,1,0:T(8,128)(2,1)} %param.9), kind=kOutput, calls=%fused_computation.17 | convolution fusion | flops 536870912 | bytes 3670020 | tf_op jit(solution)/shard_map/dot_general | solution.py:18
  15.3 0.6 iota_compare_fusion
  15.9 1.6 %collective-permute-start.2 = (bf16[1024,128]{1,0:T(8,128)(2,1)S(1)}, bf16[1024,128]{1,0:T(8,128)(2,1)S(1)}, u32[]{:S(2)}, u32[]{:S(2)}) collective-permute-start(bf16[1024,128]{1,0:T(8,128)(2,1)S(1)} %collective-permute-done), channel_id=1, source_target_pairs={{0,2},{1,3},{2,4},{3,5},{4,6},{5,7},{6,0},{7,1},{8,10},{9,11},{10,... | collective-permute-start | bytes 786440 | tf_op jit(solution)/shard_map/ppermute | solution.py:61
  17.6 1.5 %collective-permute-start.5 = (bf16[1024,128]{1,0:T(8,128)(2,1)S(1)}, bf16[1024,128]{1,0:T(8,128)(2,1)S(1)}, u32[]{:S(2)}, u32[]{:S(2)}) collective-permute-start(bf16[1024,128]{1,0:T(8,128)(2,1)S(1)} %collective-permute-done), channel_id=1, source_target_pairs={{0,1},{1,0},{2,3},{3,2},{4,5},{5,4},{6,7},{7,6},{8,9},{9,8},{10,11... | collective-permute-start | bytes 786440 | tf_op jit(solution)/shard_map/ppermute | solution.py:63
  19.1 1.4 %collective-permute-start.7 = (bf16[1024,128]{1,0:T(8,128)(2,1)S(1)}, bf16[1024,128]{1,0:T(8,128)(2,1)S(1)}, u32[]{:S(2)}, u32[]{:S(2)}) collective-permute-start(bf16[1024,128]{1,0:T(8,128)(2,1)S(1)} %collective-permute-done.3), channel_id=1, source_target_pairs={{0,2},{1,3},{2,4},{3,5},{4,6},{5,7},{6,0},{7,1},{8,10},{9,11},{10,... | collective-permute-start | bytes 786440 | tf_op jit(solution)/shard_map/ppermute | solution.py:61
  20.5 1.5 %collective-permute-start.8 = (bf16[1024,128]{1,0:T(8,128)(2,1)S(1)}, bf16[1024,128]{1,0:T(8,128)(2,1)S(1)}, u32[]{:S(2)}, u32[]{:S(2)}) collective-permute-start(bf16[1024,128]{1,0:T(8,128)(2,1)S(1)} %collective-permute-done.3), channel_id=1, source_target_pairs={{0,1},{1,0},{2,3},{3,2},{4,5},{5,4},{6,7},{7,6},{8,9},{9,8},{10,11... | collective-permute-start | bytes 786440 | tf_op jit(solution)/shard_map/ppermute | solution.py:63
  22.0 2.3 %fusion.14 = f32[1024,256]{1,0:T(8,128)S(1)} fusion(bf16[1,1024,8192]{2,1,0:T(8,128)(2,1)} %param.7, s32[]{:T(128)S(6)} %select_n.180, bf16[1024,128]{1,0:T(8,128)(2,1)S(1)} %collective-permute-done.3, bf16[1024,128]{1,0:T(8,128)(2,1)S(1)} %collective-permute-done), kind=kOutput, calls=%fused_computation.15 | convolution fusion | flops 537919488 | bytes 3670020 | tf_op jit(solution)/shard_map/dot_general | solution.py:18
  24.3 2.4 %add_add_fusion.2 = f32[1024,256]{1,0:T(8,128)S(1)} fusion(f32[1024,256]{1,0:T(8,128)S(1)} %fusion.16, f32[1024,256]{1,0:T(8,128)S(1)} %fusion.14, bf16[1,1024,8192]{2,1,0:T(8,128)(2,1)} %param.7, s32[]{:T(128)S(6)} %select_n.182, bf16[1024,128]{1,0:T(8,128)(2,1)S(1)} %collective-permute-done.4, bf16[1024,128]{1,0:T(8,128)(2,1)S(1)} %collective-permute-done.1), kind=kOutput, calls=%fused_computation.77 | convolution fusion | flops 538443776 | bytes 5767172 | tf_op jit(solution)/shard_map/dot_general | solution.py:18
  27.0 1.4 %collective-permute-start.6 = (bf16[1024,128]{1,0:T(8,128)(2,1)S(1)}, bf16[1024,128]{1,0:T(8,128)(2,1)S(1)}, u32[]{:S(2)}, u32[]{:S(2)}) collective-permute-start(bf16[1024,128]{1,0:T(8,128)(2,1)S(1)} %collective-permute-done.2), channel_id=1, source_target_pairs={{0,2},{1,3},{2,4},{3,5},{4,6},{5,7},{6,0},{7,1},{8,10},{9,11},{10,... | collective-permute-start | bytes 786440 | tf_op jit(solution)/shard_map/ppermute | solution.py:61
  29.0 3.1 %collective-permute-done.7 = bf16[1024,128]{1,0:T(8,128)(2,1)S(1)} collective-permute-done((bf16[1024,128]{1,0:T(8,128)(2,1)S(1)}, bf16[1024,128]{1,0:T(8,128)(2,1)S(1)}, u32[]{:S(2)}, u32[]{:S(2)}) %collective-permute-start.7) | collective-permute-done | bytes 262176 | tf_op jit(solution)/shard_map/ppermute | solution.py:61
  32.5 1.7 %collective-permute-start.11 = (bf16[1024,128]{1,0:T(8,128)(2,1)S(1)}, bf16[1024,128]{1,0:T(8,128)(2,1)S(1)}, u32[]{:S(2)}, u32[]{:S(2)}) collective-permute-start(bf16[1024,128]{1,0:T(8,128)(2,1)S(1)} %collective-permute-done.7), channel_id=1, source_target_pairs={{0,1},{1,0},{2,3},{3,2},{4,5},{5,4},{6,7},{7,6},{8,9},{9,8},{10,11... | collective-permute-start | bytes 786440 | tf_op jit(solution)/shard_map/ppermute | solution.py:63
  34.2 2.3 %fusion.10 = f32[1024,256]{1,0:T(8,128)S(1)} fusion(bf16[1,1024,8192]{2,1,0:T(8,128)(2,1)} %param.7, s32[]{:T(128)S(6)} %select_n.184, bf16[1024,128]{1,0:T(8,128)(2,1)S(1)} %collective-permute-done.7, bf16[1024,128]{1,0:T(8,128)(2,1)S(1)} %collective-permute-done.2), kind=kOutput, calls=%fused_computation.11 | convolution fusion | flops 537919488 | bytes 3670020 | tf_op jit(solution)/shard_map/dot_general | solution.py:18
  36.5 0.7 add_add_fusion.1
  37.2 0.8 collective-permute-done.6
  38.0 1.7 %collective-permute-start.12 = (bf16[1024,128]{1,0:T(8,128)(2,1)S(1)}, bf16[1024,128]{1,0:T(8,128)(2,1)S(1)}, u32[]{:S(2)}, u32[]{:S(2)}) collective-permute-start(bf16[1024,128]{1,0:T(8,128)(2,1)S(1)} %collective-permute-done.6), channel_id=1, source_target_pairs={{0,1},{1,0},{2,3},{3,2},{4,5},{5,4},{6,7},{7,6},{8,9},{9,8},{10,11... | collective-permute-start | bytes 786440 | tf_op jit(solution)/shard_map/ppermute | solution.py:63
  39.8 1.8 %collective-permute-done.9 = bf16[1024,128]{1,0:T(8,128)(2,1)S(1)} collective-permute-done((bf16[1024,128]{1,0:T(8,128)(2,1)S(1)}, bf16[1024,128]{1,0:T(8,128)(2,1)S(1)}, u32[]{:S(2)}, u32[]{:S(2)}) %collective-permute-start.9) | collective-permute-done | bytes 262176 | tf_op jit(solution)/shard_map/ppermute | solution.py:61
  41.6 1.5 %collective-permute-start.13 = (bf16[1024,128]{1,0:T(8,128)(2,1)S(1)}, bf16[1024,128]{1,0:T(8,128)(2,1)S(1)}, u32[]{:S(2)}, u32[]{:S(2)}) collective-permute-start(bf16[1024,128]{1,0:T(8,128)(2,1)S(1)} %collective-permute-done.9), channel_id=1, source_target_pairs={{0,1},{1,0},{2,3},{3,2},{4,5},{5,4},{6,7},{7,6},{8,9},{9,8},{10,11... | collective-permute-start | bytes 786440 | tf_op jit(solution)/shard_map/ppermute | solution.py:63
  43.1 0.7 fusion.6
  43.8 0.7 add_add_fusion
  44.6 4.4 %collective-permute-done.12 = bf16[1024,128]{1,0:T(8,128)(2,1)S(1)} collective-permute-done((bf16[1024,128]{1,0:T(8,128)(2,1)S(1)}, bf16[1024,128]{1,0:T(8,128)(2,1)S(1)}, u32[]{:S(2)}, u32[]{:S(2)}) %collective-permute-start.12) | collective-permute-done | bytes 262176 | tf_op jit(solution)/shard_map/ppermute | solution.py:63
  48.9 0.7 fusion.80
  50.1 1.7 %collective-permute-start.15 = (bf16[1024,128]{1,0:T(8,128)(2,1)S(1)}, bf16[1024,128]{1,0:T(8,128)(2,1)S(1)}, u32[]{:S(2)}, u32[]{:S(2)}) collective-permute-start(bf16[1024,128]{1,0:T(8,128)(2,1)S(1)} %fusion.80), channel_id=1, source_target_pairs={{0,1},{1,0},{2,3},{3,2},{4,5},{5,4},{6,7},{7,6},{8,9},{9,8},{10,11... | collective-permute-start | bytes 786440 | tf_op jit(solution)/shard_map/ppermute | solution.py:63
  51.8 2.8 %collective-permute-done.13 = bf16[1024,128]{1,0:T(8,128)(2,1)S(1)} collective-permute-done((bf16[1024,128]{1,0:T(8,128)(2,1)S(1)}, bf16[1024,128]{1,0:T(8,128)(2,1)S(1)}, u32[]{:S(2)}, u32[]{:S(2)}) %collective-permute-start.13) | collective-permute-done | bytes 262176 | tf_op jit(solution)/shard_map/ppermute | solution.py:63
  54.5 0.7 fusion.57
  55.7 1.7 %collective-permute-start.18 = (bf16[1024,128]{1,0:T(8,128)(2,1)S(1)}, bf16[1024,128]{1,0:T(8,128)(2,1)S(1)}, u32[]{:S(2)}, u32[]{:S(2)}) collective-permute-start(bf16[1024,128]{1,0:T(8,128)(2,1)S(1)} %fusion.57), channel_id=1, source_target_pairs={{0,1},{1,0},{2,3},{3,2},{4,5},{5,4},{6,7},{7,6},{8,9},{9,8},{10,11... | collective-permute-start | bytes 786440 | tf_op jit(solution)/shard_map/ppermute | solution.py:63
  57.4 0.8 fusion.146
  58.3 0.6 fusion.43
  58.9 1.6 %collective-permute-done.14 = bf16[1024,128]{1,0:T(8,128)(2,1)S(1)} collective-permute-done((bf16[1024,128]{1,0:T(8,128)(2,1)S(1)}, bf16[1024,128]{1,0:T(8,128)(2,1)S(1)}, u32[]{:S(2)}, u32[]{:S(2)}) %collective-permute-start.14) | collective-permute-done | bytes 262176 | tf_op jit(solution)/shard_map/ppermute | solution.py:61
  60.4 0.7 collective-permute-start.16
  61.1 1.5 %collective-permute-start.19 = (bf16[1024,128]{1,0:T(8,128)(2,1)S(1)}, bf16[1024,128]{1,0:T(8,128)(2,1)S(1)}, u32[]{:S(2)}, u32[]{:S(2)}) collective-permute-start(bf16[1024,128]{1,0:T(8,128)(2,1)S(1)} %collective-permute-done.14), channel_id=1, source_target_pairs={{0,1},{1,0},{2,3},{3,2},{4,5},{5,4},{6,7},{7,6},{8,9},{9,8},{10,11... | collective-permute-start | bytes 786440 | tf_op jit(solution)/shard_map/ppermute | solution.py:63
  62.6 3.7 %collective-permute-done.17 = bf16[1024,128]{1,0:T(8,128)(2,1)S(1)} collective-permute-done((bf16[1024,128]{1,0:T(8,128)(2,1)S(1)}, bf16[1024,128]{1,0:T(8,128)(2,1)S(1)}, u32[]{:S(2)}, u32[]{:S(2)}) %collective-permute-start.17) | collective-permute-done | bytes 262176 | tf_op jit(solution)/shard_map/ppermute | solution.py:61
  66.3 0.6 fusion.41
  67.4 1.5 %collective-permute-start.22 = (bf16[1024,128]{1,0:T(8,128)(2,1)S(1)}, bf16[1024,128]{1,0:T(8,128)(2,1)S(1)}, u32[]{:S(2)}, u32[]{:S(2)}) collective-permute-start(bf16[1024,128]{1,0:T(8,128)(2,1)S(1)} %collective-permute-done.17), channel_id=1, source_target_pairs={{0,1},{1,0},{2,3},{3,2},{4,5},{5,4},{6,7},{7,6},{8,9},{9,8},{10,11... | collective-permute-start | bytes 786440 | tf_op jit(solution)/shard_map/ppermute | solution.py:63
  69.5 2.3 %collective-permute-done.16 = bf16[1024,128]{1,0:T(8,128)(2,1)S(1)} collective-permute-done((bf16[1024,128]{1,0:T(8,128)(2,1)S(1)}, bf16[1024,128]{1,0:T(8,128)(2,1)S(1)}, u32[]{:S(2)}, u32[]{:S(2)}) %collective-permute-start.16) | collective-permute-done | bytes 262176 | tf_op jit(solution)/shard_map/ppermute | solution.py:61
  71.7 0.6 collective-permute-start.20
  72.3 1.5 %collective-permute-start.23 = (bf16[1024,128]{1,0:T(8,128)(2,1)S(1)}, bf16[1024,128]{1,0:T(8,128)(2,1)S(1)}, u32[]{:S(2)}, u32[]{:S(2)}) collective-permute-start(bf16[1024,128]{1,0:T(8,128)(2,1)S(1)} %collective-permute-done.16), channel_id=1, source_target_pairs={{0,1},{1,0},{2,3},{3,2},{4,5},{5,4},{6,7},{7,6},{8,9},{9,8},{10,11... | collective-permute-start | bytes 786440 | tf_op jit(solution)/shard_map/ppermute | solution.py:63
  73.9 3.7 %collective-permute-done.21 = bf16[1024,128]{1,0:T(8,128)(2,1)S(1)} collective-permute-done((bf16[1024,128]{1,0:T(8,128)(2,1)S(1)}, bf16[1024,128]{1,0:T(8,128)(2,1)S(1)}, u32[]{:S(2)}, u32[]{:S(2)}) %collective-permute-start.21) | collective-permute-done | bytes 262176 | tf_op jit(solution)/shard_map/ppermute | solution.py:61
  77.5 0.6 fusion.37
  78.1 0.6 collective-permute-start.24
  78.8 1.5 %collective-permute-start.25 = (bf16[1024,128]{1,0:T(8,128)(2,1)S(1)}, bf16[1024,128]{1,0:T(8,128)(2,1)S(1)}, u32[]{:S(2)}, u32[]{:S(2)}) collective-permute-start(bf16[1024,128]{1,0:T(8,128)(2,1)S(1)} %collective-permute-done.21), channel_id=1, source_target_pairs={{0,1},{1,0},{2,3},{3,2},{4,5},{5,4},{6,7},{7,6},{8,9},{9,8},{10,11... | collective-permute-start | bytes 786440 | tf_op jit(solution)/shard_map/ppermute | solution.py:63
  80.3 0.6 add_add_fusion.4
  80.9 1.9 %collective-permute-done.20 = bf16[1024,128]{1,0:T(8,128)(2,1)S(1)} collective-permute-done((bf16[1024,128]{1,0:T(8,128)(2,1)S(1)}, bf16[1024,128]{1,0:T(8,128)(2,1)S(1)}, u32[]{:S(2)}, u32[]{:S(2)}) %collective-permute-start.20) | collective-permute-done | bytes 262176 | tf_op jit(solution)/shard_map/ppermute | solution.py:61
  82.8 1.7 %collective-permute-start.26 = (bf16[1024,128]{1,0:T(8,128)(2,1)S(1)}, bf16[1024,128]{1,0:T(8,128)(2,1)S(1)}, u32[]{:S(2)}, u32[]{:S(2)}) collective-permute-start(bf16[1024,128]{1,0:T(8,128)(2,1)S(1)} %collective-permute-done.20), channel_id=1, source_target_pairs={{0,1},{1,0},{2,3},{3,2},{4,5},{5,4},{6,7},{7,6},{8,9},{9,8},{10,11... | collective-permute-start | bytes 786440 | tf_op jit(solution)/shard_map/ppermute | solution.py:63
  84.5 2.0 %collective-permute-done.24 = bf16[1024,128]{1,0:T(8,128)(2,1)S(1)} collective-permute-done((bf16[1024,128]{1,0:T(8,128)(2,1)S(1)}, bf16[1024,128]{1,0:T(8,128)(2,1)S(1)}, u32[]{:S(2)}, u32[]{:S(2)}) %collective-permute-start.24) | collective-permute-done | bytes 262176 | tf_op jit(solution)/shard_map/ppermute | solution.py:61
  86.5 1.6 %collective-permute-start.30 = (bf16[1024,128]{1,0:T(8,128)(2,1)S(1)}, bf16[1024,128]{1,0:T(8,128)(2,1)S(1)}, u32[]{:S(2)}, u32[]{:S(2)}) collective-permute-start(bf16[1024,128]{1,0:T(8,128)(2,1)S(1)} %collective-permute-done.24), channel_id=1, source_target_pairs={{0,1},{1,0},{2,3},{3,2},{4,5},{5,4},{6,7},{7,6},{8,9},{9,8},{10,11... | collective-permute-start | bytes 786440 | tf_op jit(solution)/shard_map/ppermute | solution.py:63
  88.1 0.6 fusion.33
  88.7 0.6 add_add_fusion.3
  89.3 4.6 %collective-permute-done.26 = bf16[1024,128]{1,0:T(8,128)(2,1)S(1)} collective-permute-done((bf16[1024,128]{1,0:T(8,128)(2,1)S(1)}, bf16[1024,128]{1,0:T(8,128)(2,1)S(1)}, u32[]{:S(2)}, u32[]{:S(2)}) %collective-permute-start.26) | collective-permute-done | bytes 262176 | tf_op jit(solution)/shard_map/ppermute | solution.py:63
  95.3 1.9 %collective-permute-done.30 = bf16[1024,128]{1,0:T(8,128)(2,1)S(1)} collective-permute-done((bf16[1024,128]{1,0:T(8,128)(2,1)S(1)}, bf16[1024,128]{1,0:T(8,128)(2,1)S(1)}, u32[]{:S(2)}, u32[]{:S(2)}) %collective-permute-start.30) | collective-permute-done | bytes 262176 | tf_op jit(solution)/shard_map/ppermute | solution.py:63
  99.9 1.6 %collective-permute-start.28 = (bf16[272,128]{1,0:T(8,128)(2,1)S(1)}, bf16[272,128]{1,0:T(8,128)(2,1)S(1)}, u32[]{:S(2)}, u32[]{:S(2)}) collective-permute-start(bf16[272,128]{1,0:T(8,128)(2,1)S(1)} %pad_maximum_fusion.3), channel_id=1, source_target_pairs={{0,16},{8,24},{16,0},{24,8},{1,17},{9,25},{17,1},{25,9},{2,18},{10... | collective-permute-start | bytes 208904 | tf_op jit(solution)/shard_map/ppermute | solution.py:121
  101.5 0.6 collective-permute-start.27
  102.1 1.5 %collective-permute-start.32 = (bf16[256,128]{1,0:T(8,128)(2,1)S(1)}, bf16[256,128]{1,0:T(8,128)(2,1)S(1)}, u32[]{:S(2)}, u32[]{:S(2)}) collective-permute-start(bf16[256,128]{1,0:T(8,128)(2,1)S(1)} %convolution_convert_fusion.1), channel_id=1, source_target_pairs={{0,16},{8,24},{16,0},{24,8},{1,17},{9,25},{17,1},{25,9},{2,18},{10... | collective-permute-start | bytes 196616 | tf_op jit(solution)/shard_map/ppermute | solution.py:121
  103.6 0.7 collective-permute-done.28
  104.3 1.5 %collective-permute-done.29 = bf16[272,128]{1,0:T(8,128)(2,1)S(1)} collective-permute-done((bf16[272,128]{1,0:T(8,128)(2,1)S(1)}, bf16[272,128]{1,0:T(8,128)(2,1)S(1)}, u32[]{:S(2)}, u32[]{:S(2)}) %collective-permute-start.29) | collective-permute-done | bytes 69664 | tf_op jit(solution)/shard_map/ppermute | solution.py:121
  107.3 1.2 %collective-permute-done.33 = bf16[256,128]{1,0:T(8,128)(2,1)S(1)} collective-permute-done((bf16[256,128]{1,0:T(8,128)(2,1)S(1)}, bf16[256,128]{1,0:T(8,128)(2,1)S(1)}, u32[]{:S(2)}, u32[]{:S(2)}) %collective-permute-start.33) | collective-permute-done | bytes 65568 | tf_op jit(solution)/shard_map/ppermute | solution.py:121
  109.0 0.8 maximum_bitcast_fusion
  (74 shorter events, 10.1 us)
Async XLA Ops:
  1.7 14.2 %collective-permute-start = (bf16[1024,128]{1,0:T(8,128)(2,1)S(1)}, bf16[1024,128]{1,0:T(8,128)(2,1)S(1)}, u32[]{:S(2)}, u32[]{:S(2)}) collective-permute-start(bf16[1024,128]{1,0:T(8,128)(2,1)S(1)} %get-tuple-element.64), channel_id=1, source_target_pairs={{0,2},{1,3},{2,4},{3,5},{4,6},{5,7},{6,0},{7,1},{8,10},{9,11},{10,... | collective-permute-start | bytes 786440 | tf_op jit(solution)/shard_map/ppermute | solution.py:61
  4.8 11.1 %collective-permute-start.1 = (bf16[1024,128]{1,0:T(8,128)(2,1)S(1)}, bf16[1024,128]{1,0:T(8,128)(2,1)S(1)}, u32[]{:S(2)}, u32[]{:S(2)}) collective-permute-start(bf16[1024,128]{1,0:T(8,128)(2,1)S(1)} %get-tuple-element.64), channel_id=1, source_target_pairs={{0,1},{1,0},{2,3},{3,2},{4,5},{5,4},{6,7},{7,6},{8,9},{9,8},{10,11... | collective-permute-start | bytes 786440 | tf_op jit(solution)/shard_map/ppermute | solution.py:63
  6.3 12.8 %collective-permute-start.3 = (bf16[1024,128]{1,0:T(8,128)(2,1)S(1)}, bf16[1024,128]{1,0:T(8,128)(2,1)S(1)}, u32[]{:S(2)}, u32[]{:S(2)}) collective-permute-start(bf16[1024,128]{1,0:T(8,128)(2,1)S(1)} %get-tuple-element.65), channel_id=1, source_target_pairs={{0,2},{1,3},{2,4},{3,5},{4,6},{5,7},{6,0},{7,1},{8,10},{9,11},{10,... | collective-permute-start | bytes 786440 | tf_op jit(solution)/shard_map/ppermute | solution.py:61
  7.9 11.2 %collective-permute-start.4 = (bf16[1024,128]{1,0:T(8,128)(2,1)S(1)}, bf16[1024,128]{1,0:T(8,128)(2,1)S(1)}, u32[]{:S(2)}, u32[]{:S(2)}) collective-permute-start(bf16[1024,128]{1,0:T(8,128)(2,1)S(1)} %get-tuple-element.65), channel_id=1, source_target_pairs={{0,1},{1,0},{2,3},{3,2},{4,5},{5,4},{6,7},{7,6},{8,9},{9,8},{10,11... | collective-permute-start | bytes 786440 | tf_op jit(solution)/shard_map/ppermute | solution.py:63
  15.3 21.2 %copy-start = (bf16[1,1024,8192]{2,1,0:T(8,128)(2,1)S(1)}, bf16[1,1024,8192]{2,1,0:T(8,128)(2,1)}, u32[]{:S(2)}) copy-start(bf16[1,1024,8192]{2,1,0:T(8,128)(2,1)} %param.7) | copy-start | bytes 50331652
  15.9 11.1 %collective-permute-start.2 = (bf16[1024,128]{1,0:T(8,128)(2,1)S(1)}, bf16[1024,128]{1,0:T(8,128)(2,1)S(1)}, u32[]{:S(2)}, u32[]{:S(2)}) collective-permute-start(bf16[1024,128]{1,0:T(8,128)(2,1)S(1)} %collective-permute-done), channel_id=1, source_target_pairs={{0,2},{1,3},{2,4},{3,5},{4,6},{5,7},{6,0},{7,1},{8,10},{9,11},{10,... | collective-permute-start | bytes 786440 | tf_op jit(solution)/shard_map/ppermute | solution.py:61
  17.6 9.4 %collective-permute-start.5 = (bf16[1024,128]{1,0:T(8,128)(2,1)S(1)}, bf16[1024,128]{1,0:T(8,128)(2,1)S(1)}, u32[]{:S(2)}, u32[]{:S(2)}) collective-permute-start(bf16[1024,128]{1,0:T(8,128)(2,1)S(1)} %collective-permute-done), channel_id=1, source_target_pairs={{0,1},{1,0},{2,3},{3,2},{4,5},{5,4},{6,7},{7,6},{8,9},{9,8},{10,11... | collective-permute-start | bytes 786440 | tf_op jit(solution)/shard_map/ppermute | solution.py:63
  19.1 13.0 %collective-permute-start.7 = (bf16[1024,128]{1,0:T(8,128)(2,1)S(1)}, bf16[1024,128]{1,0:T(8,128)(2,1)S(1)}, u32[]{:S(2)}, u32[]{:S(2)}) collective-permute-start(bf16[1024,128]{1,0:T(8,128)(2,1)S(1)} %collective-permute-done.3), channel_id=1, source_target_pairs={{0,2},{1,3},{2,4},{3,5},{4,6},{5,7},{6,0},{7,1},{8,10},{9,11},{10,... | collective-permute-start | bytes 786440 | tf_op jit(solution)/shard_map/ppermute | solution.py:61
  20.5 11.6 %collective-permute-start.8 = (bf16[1024,128]{1,0:T(8,128)(2,1)S(1)}, bf16[1024,128]{1,0:T(8,128)(2,1)S(1)}, u32[]{:S(2)}, u32[]{:S(2)}) collective-permute-start(bf16[1024,128]{1,0:T(8,128)(2,1)S(1)} %collective-permute-done.3), channel_id=1, source_target_pairs={{0,1},{1,0},{2,3},{3,2},{4,5},{5,4},{6,7},{7,6},{8,9},{9,8},{10,11... | collective-permute-start | bytes 786440 | tf_op jit(solution)/shard_map/ppermute | solution.py:63
  27.0 11.0 %collective-permute-start.6 = (bf16[1024,128]{1,0:T(8,128)(2,1)S(1)}, bf16[1024,128]{1,0:T(8,128)(2,1)S(1)}, u32[]{:S(2)}, u32[]{:S(2)}) collective-permute-start(bf16[1024,128]{1,0:T(8,128)(2,1)S(1)} %collective-permute-done.2), channel_id=1, source_target_pairs={{0,2},{1,3},{2,4},{3,5},{4,6},{5,7},{6,0},{7,1},{8,10},{9,11},{10,... | collective-permute-start | bytes 786440 | tf_op jit(solution)/shard_map/ppermute | solution.py:61
  28.4 15.4 %collective-permute-start.10 = (bf16[1024,128]{1,0:T(8,128)(2,1)S(1)}, bf16[1024,128]{1,0:T(8,128)(2,1)S(1)}, u32[]{:S(2)}, u32[]{:S(2)}) collective-permute-start(bf16[1024,128]{1,0:T(8,128)(2,1)S(1)} %collective-permute-done.2), channel_id=1, source_target_pairs={{0,1},{1,0},{2,3},{3,2},{4,5},{5,4},{6,7},{7,6},{8,9},{9,8},{10,11... | collective-permute-start | bytes 786440 | tf_op jit(solution)/shard_map/ppermute | solution.py:63
  32.1 9.5 %collective-permute-start.9 = (bf16[1024,128]{1,0:T(8,128)(2,1)S(1)}, bf16[1024,128]{1,0:T(8,128)(2,1)S(1)}, u32[]{:S(2)}, u32[]{:S(2)}) collective-permute-start(bf16[1024,128]{1,0:T(8,128)(2,1)S(1)} %collective-permute-done.7), channel_id=1, source_target_pairs={{0,2},{1,3},{2,4},{3,5},{4,6},{5,7},{6,0},{7,1},{8,10},{9,11},{10,... | collective-permute-start | bytes 786440 | tf_op jit(solution)/shard_map/ppermute | solution.py:61
  32.5 11.3 %collective-permute-start.11 = (bf16[1024,128]{1,0:T(8,128)(2,1)S(1)}, bf16[1024,128]{1,0:T(8,128)(2,1)S(1)}, u32[]{:S(2)}, u32[]{:S(2)}) collective-permute-start(bf16[1024,128]{1,0:T(8,128)(2,1)S(1)} %collective-permute-done.7), channel_id=1, source_target_pairs={{0,1},{1,0},{2,3},{3,2},{4,5},{5,4},{6,7},{7,6},{8,9},{9,8},{10,11... | collective-permute-start | bytes 786440 | tf_op jit(solution)/shard_map/ppermute | solution.py:63
  36.5 21.8 %slice-start = ((s8[12582912]{0:T(1024)(128)(4,1)}), s8[4194304]{0:T(1024)(128)(4,1)S(1)}, s32[]{:S(2)}) async-start(s8[12582912]{0:T(1024)(128)(4,1)} %bitcast.129), calls=%async_computation | async-start | bytes 8388608
  37.2 21.0 %slice-start.1 = ((s8[12582912]{0:T(1024)(128)(4,1)}), s8[4194304]{0:T(1024)(128)(4,1)S(1)}, s32[]{:S(2)}) async-start(s8[12582912]{0:T(1024)(128)(4,1)} %bitcast.129), calls=%async_computation.1 | async-start | bytes 8388608
  38.0 10.9 %collective-permute-start.12 = (bf16[1024,128]{1,0:T(8,128)(2,1)S(1)}, bf16[1024,128]{1,0:T(8,128)(2,1)S(1)}, u32[]{:S(2)}, u32[]{:S(2)}) collective-permute-start(bf16[1024,128]{1,0:T(8,128)(2,1)S(1)} %collective-permute-done.6), channel_id=1, source_target_pairs={{0,1},{1,0},{2,3},{3,2},{4,5},{5,4},{6,7},{7,6},{8,9},{9,8},{10,11... | collective-permute-start | bytes 786440 | tf_op jit(solution)/shard_map/ppermute | solution.py:63
  41.6 13.0 %collective-permute-start.13 = (bf16[1024,128]{1,0:T(8,128)(2,1)S(1)}, bf16[1024,128]{1,0:T(8,128)(2,1)S(1)}, u32[]{:S(2)}, u32[]{:S(2)}) collective-permute-start(bf16[1024,128]{1,0:T(8,128)(2,1)S(1)} %collective-permute-done.9), channel_id=1, source_target_pairs={{0,1},{1,0},{2,3},{3,2},{4,5},{5,4},{6,7},{7,6},{8,9},{9,8},{10,11... | collective-permute-start | bytes 786440 | tf_op jit(solution)/shard_map/ppermute | solution.py:63
  43.8 14.5 %slice-start.2 = ((s8[12582912]{0:T(1024)(128)(4,1)}), s8[4194304]{0:T(1024)(128)(4,1)S(1)}, s32[]{:S(2)}) async-start(s8[12582912]{0:T(1024)(128)(4,1)} %bitcast.129), calls=%async_computation.2 | async-start | bytes 8388608
  49.7 10.8 %collective-permute-start.14 = (bf16[1024,128]{1,0:T(8,128)(2,1)S(1)}, bf16[1024,128]{1,0:T(8,128)(2,1)S(1)}, u32[]{:S(2)}, u32[]{:S(2)}) collective-permute-start(bf16[1024,128]{1,0:T(8,128)(2,1)S(1)} %fusion.80), channel_id=1, source_target_pairs={{0,2},{1,3},{2,4},{3,5},{4,6},{5,7},{6,0},{7,1},{8,10},{9,11},{10,... | collective-permute-start | bytes 786440 | tf_op jit(solution)/shard_map/ppermute | solution.py:61
  50.1 10.3 %collective-permute-start.15 = (bf16[1024,128]{1,0:T(8,128)(2,1)S(1)}, bf16[1024,128]{1,0:T(8,128)(2,1)S(1)}, u32[]{:S(2)}, u32[]{:S(2)}) collective-permute-start(bf16[1024,128]{1,0:T(8,128)(2,1)S(1)} %fusion.80), channel_id=1, source_target_pairs={{0,1},{1,0},{2,3},{3,2},{4,5},{5,4},{6,7},{7,6},{8,9},{9,8},{10,11... | collective-permute-start | bytes 786440 | tf_op jit(solution)/shard_map/ppermute | solution.py:63
  55.3 11.0 %collective-permute-start.17 = (bf16[1024,128]{1,0:T(8,128)(2,1)S(1)}, bf16[1024,128]{1,0:T(8,128)(2,1)S(1)}, u32[]{:S(2)}, u32[]{:S(2)}) collective-permute-start(bf16[1024,128]{1,0:T(8,128)(2,1)S(1)} %fusion.57), channel_id=1, source_target_pairs={{0,2},{1,3},{2,4},{3,5},{4,6},{5,7},{6,0},{7,1},{8,10},{9,11},{10,... | collective-permute-start | bytes 786440 | tf_op jit(solution)/shard_map/ppermute | solution.py:61
  55.7 10.6 %collective-permute-start.18 = (bf16[1024,128]{1,0:T(8,128)(2,1)S(1)}, bf16[1024,128]{1,0:T(8,128)(2,1)S(1)}, u32[]{:S(2)}, u32[]{:S(2)}) collective-permute-start(bf16[1024,128]{1,0:T(8,128)(2,1)S(1)} %fusion.57), channel_id=1, source_target_pairs={{0,1},{1,0},{2,3},{3,2},{4,5},{5,4},{6,7},{7,6},{8,9},{9,8},{10,11... | collective-permute-start | bytes 786440 | tf_op jit(solution)/shard_map/ppermute | solution.py:63
  60.4 11.3 %collective-permute-start.16 = (bf16[1024,128]{1,0:T(8,128)(2,1)S(1)}, bf16[1024,128]{1,0:T(8,128)(2,1)S(1)}, u32[]{:S(2)}, u32[]{:S(2)}) collective-permute-start(bf16[1024,128]{1,0:T(8,128)(2,1)S(1)} %collective-permute-done.14), channel_id=1, source_target_pairs={{0,2},{1,3},{2,4},{3,5},{4,6},{5,7},{6,0},{7,1},{8,10},{9,11},{10,... | collective-permute-start | bytes 786440 | tf_op jit(solution)/shard_map/ppermute | solution.py:61
  61.1 10.6 %collective-permute-start.19 = (bf16[1024,128]{1,0:T(8,128)(2,1)S(1)}, bf16[1024,128]{1,0:T(8,128)(2,1)S(1)}, u32[]{:S(2)}, u32[]{:S(2)}) collective-permute-start(bf16[1024,128]{1,0:T(8,128)(2,1)S(1)} %collective-permute-done.14), channel_id=1, source_target_pairs={{0,1},{1,0},{2,3},{3,2},{4,5},{5,4},{6,7},{7,6},{8,9},{9,8},{10,11... | collective-permute-start | bytes 786440 | tf_op jit(solution)/shard_map/ppermute | solution.py:63
  66.9 10.6 %collective-permute-start.21 = (bf16[1024,128]{1,0:T(8,128)(2,1)S(1)}, bf16[1024,128]{1,0:T(8,128)(2,1)S(1)}, u32[]{:S(2)}, u32[]{:S(2)}) collective-permute-start(bf16[1024,128]{1,0:T(8,128)(2,1)S(1)} %collective-permute-done.17), channel_id=1, source_target_pairs={{0,2},{1,3},{2,4},{3,5},{4,6},{5,7},{6,0},{7,1},{8,10},{9,11},{10,... | collective-permute-start | bytes 786440 | tf_op jit(solution)/shard_map/ppermute | solution.py:61
  67.4 10.2 %collective-permute-start.22 = (bf16[1024,128]{1,0:T(8,128)(2,1)S(1)}, bf16[1024,128]{1,0:T(8,128)(2,1)S(1)}, u32[]{:S(2)}, u32[]{:S(2)}) collective-permute-start(bf16[1024,128]{1,0:T(8,128)(2,1)S(1)} %collective-permute-done.17), channel_id=1, source_target_pairs={{0,1},{1,0},{2,3},{3,2},{4,5},{5,4},{6,7},{7,6},{8,9},{9,8},{10,11... | collective-permute-start | bytes 786440 | tf_op jit(solution)/shard_map/ppermute | solution.py:63
  69.5 28.9 %copy-start.1 = (bf16[1,512,256]{2,1,0:T(8,128)(2,1)S(1)}, bf16[1,512,256]{2,1,0:T(8,128)(2,1)}, u32[]{:S(2)}) copy-start(bf16[1,512,256]{2,1,0:T(8,128)(2,1)} %param.13) | copy-start | bytes 786436
  71.7 11.1 %collective-permute-start.20 = (bf16[1024,128]{1,0:T(8,128)(2,1)S(1)}, bf16[1024,128]{1,0:T(8,128)(2,1)S(1)}, u32[]{:S(2)}, u32[]{:S(2)}) collective-permute-start(bf16[1024,128]{1,0:T(8,128)(2,1)S(1)} %collective-permute-done.16), channel_id=1, source_target_pairs={{0,2},{1,3},{2,4},{3,5},{4,6},{5,7},{6,0},{7,1},{8,10},{9,11},{10,... | collective-permute-start | bytes 786440 | tf_op jit(solution)/shard_map/ppermute | solution.py:61
  72.3 10.5 %collective-permute-start.23 = (bf16[1024,128]{1,0:T(8,128)(2,1)S(1)}, bf16[1024,128]{1,0:T(8,128)(2,1)S(1)}, u32[]{:S(2)}, u32[]{:S(2)}) collective-permute-start(bf16[1024,128]{1,0:T(8,128)(2,1)S(1)} %collective-permute-done.16), channel_id=1, source_target_pairs={{0,1},{1,0},{2,3},{3,2},{4,5},{5,4},{6,7},{7,6},{8,9},{9,8},{10,11... | collective-permute-start | bytes 786440 | tf_op jit(solution)/shard_map/ppermute | solution.py:63
  78.1 8.4 %collective-permute-start.24 = (bf16[1024,128]{1,0:T(8,128)(2,1)S(1)}, bf16[1024,128]{1,0:T(8,128)(2,1)S(1)}, u32[]{:S(2)}, u32[]{:S(2)}) collective-permute-start(bf16[1024,128]{1,0:T(8,128)(2,1)S(1)} %collective-permute-done.21), channel_id=1, source_target_pairs={{0,2},{1,3},{2,4},{3,5},{4,6},{5,7},{6,0},{7,1},{8,10},{9,11},{10,... | collective-permute-start | bytes 786440 | tf_op jit(solution)/shard_map/ppermute | solution.py:61
  78.8 9.9 %collective-permute-start.25 = (bf16[1024,128]{1,0:T(8,128)(2,1)S(1)}, bf16[1024,128]{1,0:T(8,128)(2,1)S(1)}, u32[]{:S(2)}, u32[]{:S(2)}) collective-permute-start(bf16[1024,128]{1,0:T(8,128)(2,1)S(1)} %collective-permute-done.21), channel_id=1, source_target_pairs={{0,1},{1,0},{2,3},{3,2},{4,5},{5,4},{6,7},{7,6},{8,9},{9,8},{10,11... | collective-permute-start | bytes 786440 | tf_op jit(solution)/shard_map/ppermute | solution.py:63
  82.8 11.1 %collective-permute-start.26 = (bf16[1024,128]{1,0:T(8,128)(2,1)S(1)}, bf16[1024,128]{1,0:T(8,128)(2,1)S(1)}, u32[]{:S(2)}, u32[]{:S(2)}) collective-permute-start(bf16[1024,128]{1,0:T(8,128)(2,1)S(1)} %collective-permute-done.20), channel_id=1, source_target_pairs={{0,1},{1,0},{2,3},{3,2},{4,5},{5,4},{6,7},{7,6},{8,9},{9,8},{10,11... | collective-permute-start | bytes 786440 | tf_op jit(solution)/shard_map/ppermute | solution.py:63
  86.5 10.7 %collective-permute-start.30 = (bf16[1024,128]{1,0:T(8,128)(2,1)S(1)}, bf16[1024,128]{1,0:T(8,128)(2,1)S(1)}, u32[]{:S(2)}, u32[]{:S(2)}) collective-permute-start(bf16[1024,128]{1,0:T(8,128)(2,1)S(1)} %collective-permute-done.24), channel_id=1, source_target_pairs={{0,1},{1,0},{2,3},{3,2},{4,5},{5,4},{6,7},{7,6},{8,9},{9,8},{10,11... | collective-permute-start | bytes 786440 | tf_op jit(solution)/shard_map/ppermute | solution.py:63
  99.9 4.4 %collective-permute-start.28 = (bf16[272,128]{1,0:T(8,128)(2,1)S(1)}, bf16[272,128]{1,0:T(8,128)(2,1)S(1)}, u32[]{:S(2)}, u32[]{:S(2)}) collective-permute-start(bf16[272,128]{1,0:T(8,128)(2,1)S(1)} %pad_maximum_fusion.3), channel_id=1, source_target_pairs={{0,16},{8,24},{16,0},{24,8},{1,17},{9,25},{17,1},{25,9},{2,18},{10... | collective-permute-start | bytes 208904 | tf_op jit(solution)/shard_map/ppermute | solution.py:121
  101.4 4.4 %collective-permute-start.29 = (bf16[272,128]{1,0:T(8,128)(2,1)S(1)}, bf16[272,128]{1,0:T(8,128)(2,1)S(1)}, u32[]{:S(2)}, u32[]{:S(2)}) collective-permute-start(bf16[272,128]{1,0:T(8,128)(2,1)S(1)} %pad_maximum_fusion.4), channel_id=1, source_target_pairs={{0,24},{8,16},{16,8},{24,0},{1,25},{9,17},{17,9},{25,1},{2,26},{10... | collective-permute-start | bytes 208904 | tf_op jit(solution)/shard_map/ppermute | solution.py:121
  101.5 4.3 %collective-permute-start.27 = (bf16[272,128]{1,0:T(8,128)(2,1)S(1)}, bf16[272,128]{1,0:T(8,128)(2,1)S(1)}, u32[]{:S(2)}, u32[]{:S(2)}) collective-permute-start(bf16[272,128]{1,0:T(8,128)(2,1)S(1)} %pad_maximum_fusion.2), channel_id=1, source_target_pairs={{0,8},{8,0},{16,24},{24,16},{1,9},{9,1},{17,25},{25,17},{2,10},{10... | collective-permute-start | bytes 208904 | tf_op jit(solution)/shard_map/ppermute | solution.py:121
  102.1 5.0 %collective-permute-start.32 = (bf16[256,128]{1,0:T(8,128)(2,1)S(1)}, bf16[256,128]{1,0:T(8,128)(2,1)S(1)}, u32[]{:S(2)}, u32[]{:S(2)}) collective-permute-start(bf16[256,128]{1,0:T(8,128)(2,1)S(1)} %convolution_convert_fusion.1), channel_id=1, source_target_pairs={{0,16},{8,24},{16,0},{24,8},{1,17},{9,25},{17,1},{25,9},{2,18},{10... | collective-permute-start | bytes 196616 | tf_op jit(solution)/shard_map/ppermute | solution.py:121
  103.6 5.0 %collective-permute-start.33 = (bf16[256,128]{1,0:T(8,128)(2,1)S(1)}, bf16[256,128]{1,0:T(8,128)(2,1)S(1)}, u32[]{:S(2)}, u32[]{:S(2)}) collective-permute-start(bf16[256,128]{1,0:T(8,128)(2,1)S(1)} %convolution_convert_fusion), channel_id=1, source_target_pairs={{0,24},{8,16},{16,8},{24,0},{1,25},{9,17},{17,9},{25,1},{2,26},{10... | collective-permute-start | bytes 196616 | tf_op jit(solution)/shard_map/ppermute | solution.py:121
  104.2 4.5 %collective-permute-start.31 = (bf16[256,128]{1,0:T(8,128)(2,1)S(1)}, bf16[256,128]{1,0:T(8,128)(2,1)S(1)}, u32[]{:S(2)}, u32[]{:S(2)}) collective-permute-start(bf16[256,128]{1,0:T(8,128)(2,1)S(1)} %convolution_convert_fusion.2), channel_id=1, source_target_pairs={{0,8},{8,0},{16,24},{24,16},{1,9},{9,1},{17,25},{25,17},{2,10},{10... | collective-permute-start | bytes 196616 | tf_op jit(solution)/shard_map/ppermute | solution.py:121
